TPU v7x, 256 devices: a whole 4x4x8 slice. The times are simulated.
256 devices in a mesh: patch: 64 (over x, z, core), epoch: 4 (over y).
Axes of the slice: x: 4, y: 4, z: 8, core: 2. Of those that a mesh axis runs over, the one named last changes fastest.
Arguments:
- images: bfloat16 [12288, 128, 128], P(('patch', 'epoch')), may hold values from -6 to 6
- variance: bfloat16 [12288, 128, 128], P(('patch', 'epoch')), may hold values from 0.25 to 4
- coefficients: float32 [12288, 3, 15], P(('patch', 'epoch')), may hold values from -1.8 to 1.8
- patch_of: int32 [12288, 1], P(('patch', 'epoch')), may hold values from 0 to 63; in each aligned block of 48 rows (0 to 47, 48 to 95, ...) at most 2 rows name the same one
- slot_of: int32 [12288], P(('patch', 'epoch')), may hold values from 0 to 15
Outputs:
- coadd: float32 [1024, 128, 128], P(('patch', 'epoch'))
- depth: float32 [1024, 128, 128], P(('patch', 'epoch'))
Inputs may be any that keep to these rules, and one draw needn't show every extreme that they name: `patch_of`: among the rows of one device no patch is named more than 2 times; in some device's rows one patch is named exactly 2 times.
All inputs are finite; a program needn't handle non-finite values.
Results may differ from a plain program's by a relative error of at most 0.02.
Values may be sent and summed in bfloat16 or wider, within the bound.
No kernel may reach another device: no remote copies, remote signals or barrier semaphores. Data moves between devices by JAX's collectives and lax.ppermute only.
A program may use at most 128 MiB of HBM per device.

v0:
```python
import numpy as np
import ml_dtypes
import jax
import jax.numpy as jnp
from jax import lax
from jax.experimental import pallas as pl
from jax.experimental.pallas import tpu as pltpu
from jax.sharding import Mesh, PartitionSpec as P

PIX = 128
SLOTS = 16
HELD = 48
REACH = 10
GROUPS = 16
CAP = 8
QUARTER = PIX // 4
ROWS = CAP * QUARTER
TILES_HELD = 64
STEP = 4


def band(spread, degree):
    t = np.arange(-REACH, REACH + 1)
    scaled = t.astype(np.float32) / np.float32(spread)
    taps = np.exp(np.float32(-0.5) * scaled * scaled) * scaled**degree
    taps = (taps / np.sqrt(np.sum(taps * taps))).astype(np.float32)
    out = np.zeros((PIX, PIX), np.float32)
    for k in range(PIX):
        for off, tap in zip(t, taps):
            if 0 <= k + off < PIX:
                out[k, k + off] = tap
    return out


def tables():
    bands = [band(2.0**s, d) for s in range(3) for d in range(3)]
    x_table = np.concatenate([b.T for b in bands], axis=1).astype(ml_dtypes.bfloat16)
    y_table = np.concatenate(bands, axis=1).astype(ml_dtypes.bfloat16)
    return x_table, y_table


def place_weights(patch_ref, slot_ref, var_ref, buf_ref, at_ref, weight, meta_f, meta, count, sems):
    for g in range(GROUPS):
        count[g] = 0
    meta_f[...] = jnp.zeros_like(meta_f)
    lane = lax.broadcasted_iota(jnp.int32, (16, PIX), 1)

    def copy(i, g, row):
        rows = pl.ds(pl.multiple_of(row * QUARTER, QUARTER), QUARTER)
        return pltpu.make_async_copy(weight.at[i], buf_ref.at[g, :, rows, :], sems.at[0])

    def one(i, carry):
        patch = patch_ref[i]
        x_at = patch // 16
        z_at = (patch // 2) % 8
        core = patch % 2
        g = (x_at * 2 + z_at % 2) * 2 + core
        row = count[g]
        count[g] = row + 1
        tile = (z_at // 2) * SLOTS + slot_ref[i]
        at_ref[i] = g * CAP + row
        weight[i] = (1.0 / var_ref[i].astype(jnp.float32)).astype(jnp.bfloat16).reshape(4, QUARTER, PIX)
        copy(i, g, row).start()
        mark = jnp.where(lane == row, (tile + 1).astype(jnp.float32), meta_f[g])
        meta_f[g] = jnp.where(lane == CAP, (row + 1).astype(jnp.float32), mark)
        return carry

    lax.fori_loop(0, HELD, one, 0)
    meta[...] = meta_f[...].astype(jnp.bfloat16)
    metas = [
        pltpu.make_async_copy(meta, buf_ref.at[:, q, pl.ds(ROWS, 16), :], sems.at[1 + q])
        for q in range(4)
    ]
    for m in metas:
        m.start()

    def drain(i, carry):
        copy(i, 0, 0).wait()
        return carry

    lax.fori_loop(0, HELD, drain, 0)
    for m in metas:
        m.wait()


def match_blocks(at_ref, coef_ref, img_ref, var_ref, xt_ref, yt_ref, buf_ref, z_ref, out_ref, sems):
    step = pl.program_id(0)
    last = pl.num_programs(0) - 1
    slot = lax.rem(step, 2)

    def copy(n, which, at):
        g = at // CAP
        row = at % CAP
        rows = pl.ds(pl.multiple_of(row * QUARTER, QUARTER), QUARTER)
        return pltpu.make_async_copy(out_ref.at[which, n], buf_ref.at[g, :, rows, :], sems.at[which])

    @pl.when(step >= 2)
    def _():
        for n in range(STEP):
            copy(n, slot, 0).wait()

    cols = lax.broadcasted_iota(jnp.int32, (1, PIX), 1).astype(jnp.float32)
    u = (2.0 * cols - (PIX - 1)) / (PIX - 1)
    rows = lax.broadcasted_iota(jnp.int32, (PIX, 1), 0).astype(jnp.float32)
    v = (2.0 * rows - (PIX - 1)) / (PIX - 1)
    for n in range(STEP):
        base = (step * STEP + n) * 45
        x_all = jnp.dot(img_ref[n], xt_ref[...], preferred_element_type=jnp.float32)

        def flat(b):
            return coef_ref[base + b] + coef_ref[base + 15 + b] * u

        def slope(b):
            return coef_ref[base + 30 + b]

        for s in range(3):
            b = 5 * s
            x0, x1, x2 = (x_all[:, (3 * s + d) * PIX : (3 * s + d + 1) * PIX] for d in range(3))
            parts = (
                (flat(b) * x0 + flat(b + 1) * x1 + flat(b + 3) * x2, slope(b) * x0 + slope(b + 1) * x1 + slope(b + 3) * x2),
                (flat(b + 2) * x0, slope(b + 2) * x0),
                (flat(b + 4) * x0, slope(b + 4) * x0),
            )
            for j in range(3):
                k = (3 * s + j) * PIX
                z_ref[n % 2, k : k + PIX, :PIX] = parts[j][0].astype(jnp.bfloat16)
                z_ref[n % 2, k : k + PIX, PIX:] = parts[j][1].astype(jnp.bfloat16)
        both = jnp.dot(yt_ref[...], z_ref[n % 2], preferred_element_type=jnp.float32)
        matched = both[:, :PIX] + v * both[:, PIX:]
        weighted = matched / var_ref[n].astype(jnp.float32)
        out_ref[slot, n] = weighted.astype(jnp.bfloat16).reshape(4, QUARTER, PIX)
    for n in range(STEP):
        copy(n, slot, at_ref[step * STEP + n]).start()

    @pl.when(step == last)
    def _():
        for which in (1 - slot, slot):
            for n in range(STEP):
                copy(n, which, 0).wait()


def sum_tiles(tile_ref, count_ref, got_ref, out_ref, total):
    step = pl.program_id(0)
    sources = got_ref.shape[0]

    @pl.when(step == 0)
    def _():
        total[...] = jnp.zeros_like(total)

    for n in range(sources):
        source = step * sources + n

        def add(row, carry):
            tile = tile_ref[source * CAP + row]
            rows = pl.ds(pl.multiple_of(row * QUARTER, QUARTER), QUARTER)
            total[tile] += got_ref[n, rows, :].astype(jnp.float32)
            return carry

        lax.fori_loop(0, count_ref[source], add, 0)

    @pl.when(step == pl.num_programs(0) - 1)
    def _():
        out_ref[...] = total[...].astype(jnp.bfloat16).reshape(out_ref.shape)


def tile_sums(tiles, counts, got):
    sources, rows, _ = got.shape
    each = 8
    return pl.pallas_call(
        sum_tiles,
        out_shape=jax.ShapeDtypeStruct((16, 4 * QUARTER, PIX), jnp.bfloat16),
        grid_spec=pltpu.PrefetchScalarGridSpec(
            num_scalar_prefetch=2,
            grid=(sources // each,),
            in_specs=[pl.BlockSpec((each, rows, PIX), lambda i, *_: (i, 0, 0))],
            out_specs=pl.BlockSpec((16, 4 * QUARTER, PIX), lambda i, *_: (0, 0, 0)),
            scratch_shapes=[pltpu.VMEM((TILES_HELD, QUARTER, PIX), jnp.float32)],
        ),
        compiler_params=pltpu.CompilerParams(vmem_limit_bytes=24 * 2**20),
        cost_estimate=pl.CostEstimate(flops=2 * 2**20, bytes_accessed=5 * 2**20, transcendentals=0),
    )(tiles, counts, got)


def local(images, variance, coefficients, patch_of, slot_of):
    x_table, y_table = tables()
    smem = pl.BlockSpec(memory_space=pltpu.SMEM)
    vmem = pl.BlockSpec(memory_space=pltpu.VMEM)
    anywhere = pl.BlockSpec(memory_space=pl.ANY)
    weight_buf, at = pl.pallas_call(
        place_weights,
        out_shape=(
            jax.ShapeDtypeStruct((GROUPS, 4, ROWS + 16, PIX), jnp.bfloat16),
            jax.ShapeDtypeStruct((HELD,), jnp.int32),
        ),
        in_specs=[smem, smem, vmem],
        out_specs=(anywhere, smem),
        scratch_shapes=[
            pltpu.VMEM((HELD, 4, QUARTER, PIX), jnp.bfloat16),
            pltpu.VMEM((GROUPS, 16, PIX), jnp.float32),
            pltpu.VMEM((GROUPS, 16, PIX), jnp.bfloat16),
            pltpu.SMEM((GROUPS,), jnp.int32),
            pltpu.SemaphoreType.DMA((5,)),
        ],
        compiler_params=pltpu.CompilerParams(vmem_limit_bytes=24 * 2**20),
    )(patch_of.reshape(HELD), slot_of, variance)
    group = ("x", "zl", "c", "y")
    weight_got = lax.all_to_all(
        weight_buf.reshape(64, ROWS + 16, PIX), group, split_axis=0, concat_axis=0, tiled=True
    )
    matched_buf = pl.pallas_call(
        match_blocks,
        out_shape=jax.ShapeDtypeStruct((GROUPS, 4, ROWS, PIX), jnp.bfloat16),
        grid_spec=pltpu.PrefetchScalarGridSpec(
            num_scalar_prefetch=2,
            grid=(HELD // STEP,),
            in_specs=[
                pl.BlockSpec((STEP, PIX, PIX), lambda i, *_: (i, 0, 0)),
                pl.BlockSpec((STEP, PIX, PIX), lambda i, *_: (i, 0, 0)),
                pl.BlockSpec((PIX, 9 * PIX), lambda i, *_: (0, 0)),
                pl.BlockSpec((PIX, 9 * PIX), lambda i, *_: (0, 0)),
            ],
            out_specs=anywhere,
            scratch_shapes=[
                pltpu.VMEM((2, 9 * PIX, 2 * PIX), jnp.bfloat16),
                pltpu.VMEM((2, STEP, 4, QUARTER, PIX), jnp.bfloat16),
                pltpu.SemaphoreType.DMA((2,)),
            ],
        ),
        compiler_params=pltpu.CompilerParams(vmem_limit_bytes=32 * 2**20),
        cost_estimate=pl.CostEstimate(flops=6 * 10**9, bytes_accessed=6 * 2**20, transcendentals=0),
    )(at, coefficients.reshape(-1), images, variance, jnp.asarray(x_table), jnp.asarray(y_table))
    matched_got = lax.all_to_all(
        matched_buf.reshape(64, ROWS, PIX), group, split_axis=0, concat_axis=0, tiled=True
    )
    meta = weight_got[:, ROWS, :16].astype(jnp.int32)
    tiles = (meta[:, :CAP] - 1).reshape(-1)
    counts = meta[:, CAP]
    depth_part = tile_sums(tiles, counts, weight_got)
    depth_got = lax.all_to_all(depth_part, ("zh", "y"), split_axis=0, concat_axis=0, tiled=True)
    num_part = tile_sums(tiles, counts, matched_got)
    num_got = lax.all_to_all(num_part, ("zh", "y"), split_axis=0, concat_axis=0, tiled=True)

    def whole(got):
        parts = got.reshape(4, 4, 4, QUARTER, PIX).astype(jnp.float32)
        return jnp.sum(parts, axis=0).transpose(1, 0, 2, 3).reshape(4, PIX, PIX)

    depth = whole(depth_got)
    return whole(num_got) / jnp.maximum(depth, 1.0), depth


def solution(mesh):
    names = ("x", "zh", "zl", "c", "y")
    fine = Mesh(mesh.devices.reshape(4, 4, 2, 2, 4), names)
    return jax.shard_map(
        local,
        mesh=fine,
        in_specs=(P(names, None, None), P(names, None, None), P(names, None, None), P(names, None), P(names)),
        out_specs=(P(names, None, None), P(names, None, None)),
        check_vma=False,
    )
```

profile of v0, /device:TPU:64, one launch (start us, length us, event | category | flops | bytes accessed | tf_op | source)
XLA Modules:
  0.0 181.5 jit_solution(5688842355668879976)
XLA Ops:
  0.6 0.0 copy-start.2
  0.6 1.4 copy-done.2
  2.0 0.0 copy-start.4
  2.0 0.7 copy-done.4
  2.7 0.0 copy-start.5
  2.7 0.7 copy-done.5
  3.4 3.6 %shard_map.86 = (bf16[16,4,272,128]{3,2,1,0:T(8,128)(2,1)S(1)}, s32[48]{0:T(128)S(1)}) custom-call(s32[48]{0:T(128)S(1)} %bitcast.16, s32[48]{0:T(128)S(1)} %copy-done.5, bf16[48,128,128]{2,1,0:T(8,128)(2,1)S(1)} %copy-done.2), custom_call_target="tpu_custom_call" | custom-call | tf_op jit(solution)/shard_map/pallas_call | solution.py:189
  7.0 0.0 copy-start
  7.0 2.1 %copy-done = bf16[16,4,272,128]{3,2,1,0:T(8,128)(2,1)} copy-done((bf16[16,4,272,128]{3,2,1,0:T(8,128)(2,1)}, bf16[16,4,272,128]{3,2,1,0:T(8,128)(2,1)S(1)}, u32[]{:S(2)}) %copy-start) | copy-done | bytes 4456472
  9.1 0.0 copy-start.3
  9.1 0.0 copy-start.6
  9.1 0.0 copy-start.7
  9.1 9.8 %all-to-all-start = ((bf16[64,272,128]{2,1,0:T(8,128)(2,1)}), bf16[64,272,128]{2,1,0:T(8,128)(2,1)}, u32[]{:S(2)}, u32[]{:S(2)}) async-start(bf16[64,272,128]{2,1,0:T(8,128)(2,1)} %bitcast.14), calls=%async_computation | async-start | bytes 8912896 | tf_op jit(solution)/shard_map/all_to_all | solution.py:207
  18.9 0.8 copy.11
  19.7 0.2 reshape.36.coef_ref
  19.9 0.0 copy-done.3
  20.0 0.0 copy-done.6
  20.0 0.0 copy-done.7
  20.0 0.0 copy-start.8
  20.0 1.0 copy-done.8
  20.9 16.5 %shard_map.87 = bf16[16,4,256,128]{3,2,1,0:T(8,128)(2,1)S(1)} custom-call(s32[48]{0:T(128)S(1)} %get-tuple-element.5.at_ref, f32[2160]{0:T(1024)S(1)} %reshape.36.coef_ref, bf16[48,128,128]{2,1,0:T(8,128)(2,1)S(1)} %copy-done.6, bf16[48,128,128]{2,1,0:T(8,128)(2,1)S(1)} %copy-done.3, bf16[128,1152]{1,0:T(8,128)(2,1)S(1)} %copy-done.7, ...), custom_call_target="tpu_custom_call" | custom-call | flops 6000000000 | bytes 6291456 | tf_op jit(solution)/shard_map/pallas_call | solution.py:210
  37.4 0.0 copy-start.1
  37.4 2.0 %copy-done.1 = bf16[16,4,256,128]{3,2,1,0:T(8,128)(2,1)} copy-done((bf16[16,4,256,128]{3,2,1,0:T(8,128)(2,1)}, bf16[16,4,256,128]{3,2,1,0:T(8,128)(2,1)S(1)}, u32[]{:S(2)}) %copy-start.1) | copy-done | bytes 4194328
  39.4 32.9 %all-to-all-done.got_ref = bf16[64,272,128]{2,1,0:T(8,128)(2,1)} async-done(((bf16[64,272,128]{2,1,0:T(8,128)(2,1)}), bf16[64,272,128]{2,1,0:T(8,128)(2,1)}, u32[]{:S(2)}, u32[]{:S(2)}) %all-to-all-start) | async-done | bytes 4456480 | tf_op jit(solution)/shard_map/all_to_all | solution.py:207
  72.4 8.3 %all-to-all-start.1 = ((bf16[64,256,128]{2,1,0:T(8,128)(2,1)}), bf16[64,256,128]{2,1,0:T(8,128)(2,1)}, u32[]{:S(2)}, u32[]{:S(2)}) async-start(bf16[64,256,128]{2,1,0:T(8,128)(2,1)} %bitcast.15), calls=%async_computation.1 | async-start | bytes 8388608 | tf_op jit(solution)/shard_map/all_to_all | solution.py:232
  80.6 0.9 slice_convert_fusion
  81.6 0.1 reshape.35.tile_ref
  81.7 0.2 slice_reduce_fusion.count_ref
  81.9 7.4 %shard_map.89 = bf16[16,128,128]{2,1,0:T(8,128)(2,1)} custom-call(s32[512]{0:T(512)S(1)} %reshape.35.tile_ref, s32[64]{0:T(128)S(1)} %slice_reduce_fusion.count_ref, bf16[64,272,128]{2,1,0:T(8,128)(2,1)} %all-to-all-done.got_ref), custom_call_target="tpu_custom_call" | custom-call | flops 2097152 | bytes 5242880 | tf_op jit(solution)/shard_map/pallas_call | solution.py:169
  89.3 41.9 %all-to-all-done.1.got_ref = bf16[64,256,128]{2,1,0:T(8,128)(2,1)} async-done(((bf16[64,256,128]{2,1,0:T(8,128)(2,1)}), bf16[64,256,128]{2,1,0:T(8,128)(2,1)}, u32[]{:S(2)}, u32[]{:S(2)}) %all-to-all-start.1) | async-done | bytes 4194336 | tf_op jit(solution)/shard_map/all_to_all | solution.py:232
  131.2 12.2 %all-to-all-start.3 = ((bf16[16,128,128]{2,1,0:T(8,128)(2,1)}), bf16[16,128,128]{2,1,0:T(8,128)(2,1)S(1)}, u32[]{:S(2)}, u32[]{:S(2)}) async-start(bf16[16,128,128]{2,1,0:T(8,128)(2,1)} %shard_map.89), calls=%async_computation.3 | async-start | bytes 1048576 | tf_op jit(solution)/shard_map/all_to_all | solution.py:239
  143.4 7.3 %shard_map.88 = bf16[16,128,128]{2,1,0:T(8,128)(2,1)} custom-call(s32[512]{0:T(512)S(1)} %reshape.35.tile_ref, s32[64]{0:T(128)S(1)} %slice_reduce_fusion.count_ref, bf16[64,256,128]{2,1,0:T(8,128)(2,1)} %all-to-all-done.1.got_ref), custom_call_target="tpu_custom_call" | custom-call | flops 2097152 | bytes 5242880 | tf_op jit(solution)/shard_map/pallas_call | solution.py:169
  150.7 3.8 %all-to-all-done.3 = bf16[16,128,128]{2,1,0:T(8,128)(2,1)S(1)} async-done(((bf16[16,128,128]{2,1,0:T(8,128)(2,1)}), bf16[16,128,128]{2,1,0:T(8,128)(2,1)S(1)}, u32[]{:S(2)}, u32[]{:S(2)}) %all-to-all-start.3) | async-done | bytes 524320 | tf_op jit(solution)/shard_map/all_to_all | solution.py:239
  154.5 9.8 %all-to-all-start.2 = ((bf16[16,128,128]{2,1,0:T(8,128)(2,1)}), bf16[16,128,128]{2,1,0:T(8,128)(2,1)S(1)}, u32[]{:S(2)}, u32[]{:S(2)}) async-start(bf16[16,128,128]{2,1,0:T(8,128)(2,1)} %shard_map.88), calls=%async_computation.2 | async-start | bytes 1048576 | tf_op jit(solution)/shard_map/all_to_all | solution.py:241
  164.3 0.1 convert_reduce_fusion
  164.4 0.0 copy-start.9
  164.4 16.2 %all-to-all-done.2 = bf16[16,128,128]{2,1,0:T(8,128)(2,1)S(1)} async-done(((bf16[16,128,128]{2,1,0:T(8,128)(2,1)}), bf16[16,128,128]{2,1,0:T(8,128)(2,1)S(1)}, u32[]{:S(2)}, u32[]{:S(2)}) %all-to-all-start.2) | async-done | bytes 524320 | tf_op jit(solution)/shard_map/all_to_all | solution.py:241
  180.6 0.1 convert_reduce_fusion.1
  180.7 0.8 bitcast_divide_fusion
  181.5 0.0 copy-done.9
  (3 shorter events, 0.0 us)
Async XLA Ops:
  0.6 1.4 copy-start.2
  2.0 0.7 copy-start.4
  2.7 0.7 copy-start.5
  7.0 2.1 %copy-start = (bf16[16,4,272,128]{3,2,1,0:T(8,128)(2,1)}, bf16[16,4,272,128]{3,2,1,0:T(8,128)(2,1)S(1)}, u32[]{:S(2)}) copy-start(bf16[16,4,272,128]{3,2,1,0:T(8,128)(2,1)S(1)} %get-tuple-element.4) | copy-start | bytes 13369348
  9.1 10.9 %copy-start.3 = (bf16[48,128,128]{2,1,0:T(8,128)(2,1)S(1)}, bf16[48,128,128]{2,1,0:T(8,128)(2,1)}, u32[]{:S(2)}) copy-start(bf16[48,128,128]{2,1,0:T(8,128)(2,1)} %var_ref.3) | copy-start | bytes 4718596
  9.1 10.9 %copy-start.6 = (bf16[48,128,128]{2,1,0:T(8,128)(2,1)S(1)}, bf16[48,128,128]{2,1,0:T(8,128)(2,1)}, u32[]{:S(2)}) copy-start(bf16[48,128,128]{2,1,0:T(8,128)(2,1)} %img_ref.1) | copy-start | bytes 4718596
  9.1 10.9 %copy-start.7 = (bf16[128,1152]{1,0:T(8,128)(2,1)S(1)}, bf16[128,1152]{1,0:T(8,128)(2,1)}, u32[]{:S(2)}) copy-start(bf16[128,1152]{1,0:T(8,128)(2,1)} %constant.11.clone.xt_ref) | copy-start | bytes 884740
  9.1 63.3 %all-to-all-start = ((bf16[64,272,128]{2,1,0:T(8,128)(2,1)}), bf16[64,272,128]{2,1,0:T(8,128)(2,1)}, u32[]{:S(2)}, u32[]{:S(2)}) async-start(bf16[64,272,128]{2,1,0:T(8,128)(2,1)} %bitcast.14), calls=%async_computation | async-start | bytes 8912896 | tf_op jit(solution)/shard_map/all_to_all | solution.py:207
  20.0 1.0 copy-start.8
  37.4 2.0 %copy-start.1 = (bf16[16,4,256,128]{3,2,1,0:T(8,128)(2,1)}, bf16[16,4,256,128]{3,2,1,0:T(8,128)(2,1)S(1)}, u32[]{:S(2)}) copy-start(bf16[16,4,256,128]{3,2,1,0:T(8,128)(2,1)S(1)} %shard_map.87) | copy-start | bytes 12582916
  72.4 58.8 %all-to-all-start.1 = ((bf16[64,256,128]{2,1,0:T(8,128)(2,1)}), bf16[64,256,128]{2,1,0:T(8,128)(2,1)}, u32[]{:S(2)}, u32[]{:S(2)}) async-start(bf16[64,256,128]{2,1,0:T(8,128)(2,1)} %bitcast.15), calls=%async_computation.1 | async-start | bytes 8388608 | tf_op jit(solution)/shard_map/all_to_all | solution.py:232
  131.2 23.3 %all-to-all-start.3 = ((bf16[16,128,128]{2,1,0:T(8,128)(2,1)}), bf16[16,128,128]{2,1,0:T(8,128)(2,1)S(1)}, u32[]{:S(2)}, u32[]{:S(2)}) async-start(bf16[16,128,128]{2,1,0:T(8,128)(2,1)} %shard_map.89), calls=%async_computation.3 | async-start | bytes 1048576 | tf_op jit(solution)/shard_map/all_to_all | solution.py:239
  154.5 26.1 %all-to-all-start.2 = ((bf16[16,128,128]{2,1,0:T(8,128)(2,1)}), bf16[16,128,128]{2,1,0:T(8,128)(2,1)S(1)}, u32[]{:S(2)}, u32[]{:S(2)}) async-start(bf16[16,128,128]{2,1,0:T(8,128)(2,1)} %shard_map.88), calls=%async_computation.2 | async-start | bytes 1048576 | tf_op jit(solution)/shard_map/all_to_all | solution.py:241
  164.4 17.0 %copy-start.9 = (f32[4,4,32,128]{3,2,1,0:T(8,128)}, f32[4,4,32,128]{3,2,1,0:T(8,128)S(1)}, u32[]{:S(2)}) copy-start(f32[4,4,32,128]{3,2,1,0:T(8,128)S(1)} %copy.13) | copy-start | bytes 786436
where the time goes:
time: 182 us; the launch traced here: 181 us
  waiting for transfers between devices  94.8 us (52%)
  starting transfers between devices  40.1 us (22%)
  Pallas kernels  34.8 us (19%)
  local copies, waits for them, and re-layouts  9.17 us (5%)
  other arithmetic  1.83 us (1%)
    all_to_all x1, waiting for transfers between devices, local(): lax.all_to_all(matched_buf.reshape(64, ROWS, PIX), group, split_axis=0, c...  41.9 us
    all_to_all x1, waiting for transfers between devices, local(): lax.all_to_all(weight_buf.reshape(64, ROWS + 16, PIX), group, split_axis=...  32.9 us
    pallas_call x1, Pallas kernels, local(): pl.pallas_call(match_blocks, out_shape=jax.ShapeDtypeStruct((GROUPS, 4, R...  16.5 us
    all_to_all x1, waiting for transfers between devices, local(): lax.all_to_all(num_part, ('zh', 'y'), split_axis=0, concat_axis=0, tiled=...  16.2 us
    pallas_call x2, Pallas kernels, tile_sums(): pl.pallas_call(sum_tiles, out_shape=jax.ShapeDtypeStruct((16, 4 * QUARTER...  14.7 us
    all_to_all x1, starting transfers between devices, local(): lax.all_to_all(depth_part, ('zh', 'y'), split_axis=0, concat_axis=0, tile...  12.2 us
    all_to_all x1, starting transfers between devices, local(): lax.all_to_all(num_part, ('zh', 'y'), split_axis=0, concat_axis=0, tiled=...  9.85 us
    all_to_all x1, starting transfers between devices, local(): lax.all_to_all(weight_buf.reshape(64, ROWS + 16, PIX), group, split_axis=...  9.79 us
  transfers between devices with their start and end apart: 4, of which 4 were waited for; matrix products, arithmetic and copies ran while one was open for 1% of the time, Pallas kernels for 17%

commit v1 on v0

v1 whole, which is shorter than its diff:
```python
import numpy as np
import ml_dtypes
import jax
import jax.numpy as jnp
from jax import lax
from jax.experimental import pallas as pl
from jax.experimental.pallas import tpu as pltpu
from jax.sharding import Mesh, PartitionSpec as P

PIX = 128
SLOTS = 16
HELD = 48
REACH = 10
GROUP = 64
PARTS = 4
ROWS = PARTS * HELD
META = 16
ALL_BLOCKS = GROUP * HELD
TILES = 256
STEP = 4
LOADS = 4
PARAMS = pltpu.CompilerParams(vmem_limit_bytes=56 * 2**20)

VMEM_SPEC = pl.BlockSpec(memory_space=pltpu.VMEM)
HBM_SPEC = pl.BlockSpec(memory_space=pltpu.HBM)


def band(spread, degree):
    t = np.arange(-REACH, REACH + 1)
    scaled = t.astype(np.float32) / np.float32(spread)
    taps = np.exp(np.float32(-0.5) * scaled * scaled) * scaled**degree
    taps = (taps / np.sqrt(np.sum(taps * taps))).astype(np.float32)
    out = np.zeros((PIX, PIX), np.float32)
    for k in range(PIX):
        for off, tap in zip(t, taps):
            if 0 <= k + off < PIX:
                out[k, k + off] = tap
    return out


def tables():
    bands = [band(2.0**s, d) for s in range(3) for d in range(3)]
    x_table = np.concatenate([b.T for b in bands], axis=1).astype(ml_dtypes.bfloat16)
    y_table = np.concatenate(bands, axis=1).astype(ml_dtypes.bfloat16)
    return x_table, y_table


def match_blocks(coef_ref, img_ref, var_ref, xt_ref, yt_ref, meta_ref, out_hbm, z_ref, staged, packed, sems):
    step = pl.program_id(0)
    last = pl.num_programs(0) - 1

    def put(part, i, value):
        staged[pl.ds(part * HELD + i, GROUP, stride=ROWS), :] = value

    cols = lax.broadcasted_iota(jnp.int32, (1, PIX), 1).astype(jnp.float32)
    u = (2.0 * cols - (PIX - 1)) / (PIX - 1)
    rows = lax.broadcasted_iota(jnp.int32, (PIX, 1), 0).astype(jnp.float32)
    v = (2.0 * rows - (PIX - 1)) / (PIX - 1)
    for n in range(STEP):
        base = (step * STEP + n) * 45
        x_all = jnp.dot(img_ref[n], xt_ref[...], preferred_element_type=jnp.float32)

        def flat(b):
            return coef_ref[base + b] + coef_ref[base + 15 + b] * u

        def slope(b):
            return coef_ref[base + 30 + b]

        for s in range(3):
            b = 5 * s
            x0, x1, x2 = (x_all[:, (3 * s + d) * PIX : (3 * s + d + 1) * PIX] for d in range(3))
            parts = (
                (flat(b) * x0 + flat(b + 1) * x1 + flat(b + 3) * x2, slope(b) * x0 + slope(b + 1) * x1 + slope(b + 3) * x2),
                (flat(b + 2) * x0, slope(b + 2) * x0),
                (flat(b + 4) * x0, slope(b + 4) * x0),
            )
            for j in range(3):
                k = (3 * s + j) * PIX
                z_ref[n % 2, k : k + PIX, :PIX] = parts[j][0].astype(jnp.bfloat16)
                z_ref[n % 2, k : k + PIX, PIX:] = parts[j][1].astype(jnp.bfloat16)
        both = jnp.dot(yt_ref[...], z_ref[n % 2], preferred_element_type=jnp.float32)
        matched = both[:, :PIX] + v * both[:, PIX:]
        weight = 1.0 / var_ref[n].astype(jnp.float32)
        weighted = matched * weight
        i = step * STEP + n
        put(0, i, weight[:GROUP])
        put(1, i, weight[GROUP:])
        put(2, i, weighted[:GROUP])
        put(3, i, weighted[GROUP:])

    @pl.when(step == last)
    def _():
        copies = []
        each = GROUP // 8
        for k in range(8):
            for d in range(k * each, (k + 1) * each):
                packed[d, :ROWS, :] = staged[d * ROWS : (d + 1) * ROWS, :].astype(jnp.bfloat16)
                packed[d, ROWS:, :] = meta_ref[...]
            at = pl.ds(k * each, each)
            copies.append(pltpu.make_async_copy(packed.at[at], out_hbm.at[at], sems.at[k]))
            copies[-1].start()
        for c in copies:
            c.wait()


def sum_tiles(id_ref, got_hbm, *refs):
    outs, (blocks, hot, sems) = refs[:4], refs[4:]
    held = GROUP // LOADS
    loads = []
    for n in range(LOADS):
        at = pl.ds(n * held, held)
        for part in range(PARTS):
            src = got_hbm.at[at, pl.ds(part * HELD, HELD), :]
            dst = blocks.at[at, :, pl.ds(part * PIX, PIX)]
            loads.append(pltpu.make_async_copy(src, dst, sems.at[n * PARTS + part]))
    for c in loads:
        c.start()
    tile = lax.broadcasted_iota(jnp.int32, (TILES, PIX), 0)
    for m, out in enumerate(outs):
        for k in range(ALL_BLOCKS // PIX):
            ids = id_ref[k : k + 1, :]
            hot[:, k * PIX : (k + 1) * PIX] = jnp.where(ids == tile + m * TILES, 1.0, 0.0).astype(jnp.bfloat16)
        if m == 0:
            for c in loads:
                c.wait()
        values = blocks[...].reshape(ALL_BLOCKS, PARTS * PIX)
        out[...] = jnp.dot(hot[...], values, preferred_element_type=jnp.float32).astype(jnp.bfloat16)


def add_halves(a_ref, b_ref, c_ref, d_ref, out_ref, turned):
    total = sum(ref[...].astype(jnp.float32) for ref in (a_ref, b_ref, c_ref, d_ref))
    for part in range(PARTS):
        for s in range(4):
            turned[pl.ds(part * 4 + s, GROUP, stride=16), :] = total[s * GROUP : (s + 1) * GROUP, part * PIX : (part + 1) * PIX]
    out_ref[...] = turned[...].astype(jnp.bfloat16).reshape(GROUP, 16, PIX)


def combine(got_ref, coadd_ref, depth_ref, flat):
    flat[...] = got_ref[...].astype(jnp.float32).reshape(GROUP * 16, PIX)
    for s in range(4):
        for half in range(2):
            rows = slice(half * GROUP, (half + 1) * GROUP)
            depth = flat[pl.ds(half * 4 + s, GROUP, stride=16), :]
            num = flat[pl.ds((2 + half) * 4 + s, GROUP, stride=16), :]
            depth_ref[s, rows, :] = depth
            coadd_ref[s, rows, :] = num / jnp.maximum(depth, 1.0)


def local(images, variance, coefficients, patch_of, slot_of):
    x_table, y_table = tables()
    patch = patch_of.reshape(HELD)
    z_at = (patch // 2) % 8
    owner = ((patch // 16 * 2 + z_at % 2) * 2 + patch % 2) * 4 + slot_of // 4
    z_by = (z_at // 2 - lax.axis_index("zh")) % 4
    tile = jnp.pad((z_by * 4 + slot_of % 4) * GROUP + owner, (0, PIX - HELD))
    code = jnp.stack([tile % PIX, tile // PIX]).astype(jnp.bfloat16)
    meta = jnp.broadcast_to(code[:, None, :], (2, META // 2, PIX)).reshape(META, PIX)
    buf = pl.pallas_call(
        match_blocks,
        out_shape=jax.ShapeDtypeStruct((GROUP, ROWS + META, PIX), jnp.bfloat16),
        grid_spec=pltpu.PrefetchScalarGridSpec(
            num_scalar_prefetch=1,
            grid=(HELD // STEP,),
            in_specs=[
                pl.BlockSpec((STEP, PIX, PIX), lambda i, *_: (i, 0, 0)),
                pl.BlockSpec((STEP, PIX, PIX), lambda i, *_: (i, 0, 0)),
                pl.BlockSpec((PIX, 9 * PIX), lambda i, *_: (0, 0)),
                pl.BlockSpec((PIX, 9 * PIX), lambda i, *_: (0, 0)),
                pl.BlockSpec((META, PIX), lambda i, *_: (0, 0)),
            ],
            out_specs=HBM_SPEC,
            scratch_shapes=[
                pltpu.VMEM((2, 9 * PIX, 2 * PIX), jnp.bfloat16),
                pltpu.VMEM((GROUP * ROWS, PIX), jnp.float32),
                pltpu.VMEM((GROUP, ROWS + META, PIX), jnp.bfloat16),
                pltpu.SemaphoreType.DMA((8,)),
            ],
        ),
        compiler_params=PARAMS,
    )(coefficients.reshape(-1), images, variance, jnp.asarray(x_table), jnp.asarray(y_table), meta)
    group = ("x", "zl", "c", "y")
    got = lax.all_to_all(buf, group, split_axis=0, concat_axis=0, tiled=True)
    code = got[:, ROWS :: META // 2, :HELD].astype(jnp.int32)
    ids = (code[:, 0] + PIX * code[:, 1]).reshape(ALL_BLOCKS // PIX, PIX)
    part = jax.ShapeDtypeStruct((TILES, PARTS * PIX), jnp.bfloat16)
    parts = pl.pallas_call(
        sum_tiles,
        out_shape=[part] * 4,
        in_specs=[VMEM_SPEC, HBM_SPEC],
        out_specs=[VMEM_SPEC] * 4,
        scratch_shapes=[
            pltpu.VMEM((GROUP, HELD, PARTS * PIX), jnp.bfloat16),
            pltpu.VMEM((TILES, ALL_BLOCKS), jnp.bfloat16),
            pltpu.SemaphoreType.DMA((LOADS * PARTS,)),
        ],
        compiler_params=PARAMS,
    )(ids, got)
    moved = [lax.ppermute(parts[by], "zh", [(i, (i + by) % 4) for i in range(4)]) for by in (2, 1, 3)]
    summed = pl.pallas_call(
        add_halves,
        out_shape=jax.ShapeDtypeStruct((GROUP, 16, PIX), jnp.bfloat16),
        in_specs=[VMEM_SPEC] * 4,
        out_specs=VMEM_SPEC,
        scratch_shapes=[pltpu.VMEM((GROUP * 16, PIX), jnp.float32)],
        compiler_params=PARAMS,
    )(parts[0], *moved)
    whole = lax.all_to_all(summed, group, split_axis=0, concat_axis=0, tiled=True)
    out = jax.ShapeDtypeStruct((4, PIX, PIX), jnp.float32)
    return pl.pallas_call(
        combine,
        out_shape=(out, out),
        in_specs=[VMEM_SPEC],
        out_specs=(VMEM_SPEC, VMEM_SPEC),
        scratch_shapes=[pltpu.VMEM((GROUP * 16, PIX), jnp.float32)],
        compiler_params=PARAMS,
    )(whole)


def solution(mesh):
    names = ("x", "zh", "zl", "c", "y")
    fine = Mesh(mesh.devices.reshape(4, 4, 2, 2, 4), names)
    return jax.shard_map(
        local,
        mesh=fine,
        in_specs=(P(names, None, None), P(names, None, None), P(names, None, None), P(names, None), P(names)),
        out_specs=(P(names, None, None), P(names, None, None)),
        check_vma=False,
    )
```

time: 182 us -> 138 us (0.76)
  the two profiles are of different devices: /device:TPU:64 before, /device:TPU:1 now
where the time goes in v1:
time: 138 us
  blocking collectives  67.4 us (49%)
  Pallas kernels  33.2 us (24%)
  waiting for transfers between devices  21.1 us (15%)
  starting transfers between devices  9.68 us (7%)
  local copies, waits for them, and re-layouts  4.73 us (3%)
    all_to_all x1, blocking collectives, local(): got = lax.all_to_all(buf, group, split_axis=0, concat_axis=0, tiled=True)  52.5 us
    pallas_call x1, Pallas kernels, local(): pl.pallas_call(match_blocks, out_shape=jax.ShapeDtypeStruct((GROUP, ROWS...  21.9 us
    ppermute x3, waiting for transfers between devices, local(): lax.ppermute(parts[by], 'zh', [(i, (i + by) % 4) for i in range(4)])  21.1 us
    all_to_all x1, blocking collectives, local(): lax.all_to_all(summed, group, split_axis=0, concat_axis=0, tiled=True)  14.9 us
    ppermute x3, starting transfers between devices, local(): lax.ppermute(parts[by], 'zh', [(i, (i + by) % 4) for i in range(4)])  9.68 us
    pallas_call x1, Pallas kernels, local(): pl.pallas_call(sum_tiles, out_shape=[part] * 4, in_specs=[VMEM_SPEC, HBM_...  7.2 us
  transfers between devices with their start and end apart: 3, of which 3 were waited for; matrix products, arithmetic and copies ran while one was open for 0% of the time, Pallas kernels for 0%

profile of v1, /device:TPU:1, one launch (start us, length us, event | category | flops | bytes accessed | tf_op | source)
XLA Modules:
  0.0 137.8 jit_solution(16194095710008268572)
XLA Ops:
  0.6 0.7 add_add_fusion
  1.4 0.6 broadcast_bitcast_fusion.meta_ref
  2.0 0.8 copy.9
  2.8 0.8 reshape.38.coef_ref
  3.6 21.9 %shard_map.86 = bf16[64,208,128]{2,1,0:T(8,128)(2,1)} custom-call(f32[2160]{0:T(1024)} %reshape.38.coef_ref, bf16[48,128,128]{2,1,0:T(8,128)(2,1)} %img_ref.1, bf16[48,128,128]{2,1,0:T(8,128)(2,1)} %var_ref.1, bf16[128,1152]{1,0:T(8,128)(2,1)} %constant.123.clone.xt_ref, bf16[128,1152]{1,0:T(8,128)(2,1)} %constant.124.clone.yt_ref, ...), custom_call_target="tpu_custom_call" | custom-call | tf_op jit(solution)/shard_map/pallas_call | solution.py:158
  25.6 52.5 %all_to_all.10.got_hbm = bf16[64,208,128]{2,1,0:T(8,128)(2,1)S(1)} all-to-all(bf16[64,208,128]{2,1,0:T(8,128)(2,1)} %shard_map.86), channel_id=1, replica_groups=mesh['x'=4,'zh'=4,'zl'=2,'c'=2,'y'=4] {'x','zl','c','y'}, dimensions={0} | all-to-all | bytes 6815744 | tf_op jit(solution)/shard_map/all_to_all | solution.py:182
  78.1 0.0 copy-start
  78.1 1.1 slice.9
  79.2 0.1 fusion.1
  79.4 0.7 add.69.id_ref
  80.0 0.0 copy-done
  80.0 7.2 %shard_map.87 = (bf16[256,512]{1,0:T(8,128)(2,1)}, bf16[256,512]{1,0:T(8,128)(2,1)}, bf16[256,512]{1,0:T(8,128)(2,1)}, bf16[256,512]{1,0:T(8,128)(2,1)}) custom-call(s32[24,128]{1,0:T(8,128)} %add.69.id_ref, bf16[64,208,128]{2,1,0:T(8,128)(2,1)} %copy-done), custom_call_target="tpu_custom_call" | custom-call | tf_op jit(solution)/shard_map/pallas_call | solution.py:186
  87.3 6.1 %collective-permute-start = (bf16[256,512]{1,0:T(8,128)(2,1)}, bf16[256,512]{1,0:T(8,128)(2,1)S(1)}, u32[]{:S(2)}, u32[]{:S(2)}) collective-permute-start(bf16[256,512]{1,0:T(8,128)(2,1)} %get-tuple-element.7), channel_id=1, source_target_pairs={{0,32},{16,48},{32,0},{48,16},{1,33},{17,49},{33,1},{49,17},{2,34}... | collective-permute-start | bytes 786440 | tf_op jit(solution)/shard_map/ppermute | solution.py:198
  93.4 1.2 collective-permute-start.1
  94.6 2.4 %collective-permute-start.2 = (bf16[256,512]{1,0:T(8,128)(2,1)}, bf16[256,512]{1,0:T(8,128)(2,1)S(1)}, u32[]{:S(2)}, u32[]{:S(2)}) collective-permute-start(bf16[256,512]{1,0:T(8,128)(2,1)} %get-tuple-element.9), channel_id=1, source_target_pairs={{0,48},{16,0},{32,16},{48,32},{1,49},{17,1},{33,17},{49,33},{2,50}... | collective-permute-start | bytes 786440 | tf_op jit(solution)/shard_map/ppermute | solution.py:198
  96.9 1.7 %collective-permute-done.b_ref = bf16[256,512]{1,0:T(8,128)(2,1)S(1)} collective-permute-done((bf16[256,512]{1,0:T(8,128)(2,1)}, bf16[256,512]{1,0:T(8,128)(2,1)S(1)}, u32[]{:S(2)}, u32[]{:S(2)}) %collective-permute-start) | collective-permute-done | bytes 262176 | tf_op jit(solution)/shard_map/ppermute | solution.py:198
  98.7 0.0 copy-start.1
  98.7 13.3 %collective-permute-done.1.c_ref = bf16[256,512]{1,0:T(8,128)(2,1)S(1)} collective-permute-done((bf16[256,512]{1,0:T(8,128)(2,1)}, bf16[256,512]{1,0:T(8,128)(2,1)S(1)}, u32[]{:S(2)}, u32[]{:S(2)}) %collective-permute-start.1) | collective-permute-done | bytes 262176 | tf_op jit(solution)/shard_map/ppermute | solution.py:198
  112.0 0.0 copy-start.2
  112.0 6.1 %collective-permute-done.2.d_ref = bf16[256,512]{1,0:T(8,128)(2,1)S(1)} collective-permute-done((bf16[256,512]{1,0:T(8,128)(2,1)}, bf16[256,512]{1,0:T(8,128)(2,1)S(1)}, u32[]{:S(2)}, u32[]{:S(2)}) %collective-permute-start.2) | collective-permute-done | bytes 262176 | tf_op jit(solution)/shard_map/ppermute | solution.py:198
  118.0 0.0 copy-start.3
  118.0 0.0 copy-done.1
  118.0 0.0 copy-done.2
  118.0 0.7 copy-done.3
  118.7 2.2 %shard_map.88 = bf16[64,16,128]{2,1,0:T(8,128)(2,1)} custom-call(bf16[256,512]{1,0:T(8,128)(2,1)} %get-tuple-element.6.a_ref, bf16[256,512]{1,0:T(8,128)(2,1)} %copy-done.1, bf16[256,512]{1,0:T(8,128)(2,1)} %copy-done.2, bf16[256,512]{1,0:T(8,128)(2,1)} %copy-done.3), custom_call_target="tpu_custom_call" | custom-call | tf_op jit(solution)/shard_map/pallas_call | solution.py:199
  121.0 14.9 %all_to_all.11.got_ref = bf16[64,16,128]{2,1,0:T(8,128)(2,1)} all-to-all(bf16[64,16,128]{2,1,0:T(8,128)(2,1)} %shard_map.88), channel_id=1, replica_groups=mesh['x'=4,'zh'=4,'zl'=2,'c'=2,'y'=4] {'x','zl','c','y'}, dimensions={0} | all-to-all | bytes 524288 | tf_op jit(solution)/shard_map/all_to_all | solution.py:207
  135.9 1.9 %shard_map.89 = (f32[4,128,128]{2,1,0:T(8,128)}, f32[4,128,128]{2,1,0:T(8,128)}) custom-call(bf16[64,16,128]{2,1,0:T(8,128)(2,1)} %all_to_all.11.got_ref), custom_call_target="tpu_custom_call" | custom-call | tf_op jit(solution)/shard_map/pallas_call | solution.py:209
  (4 shorter events, 0.1 us)
Async XLA Ops:
  78.1 1.9 %copy-start = (bf16[64,208,128]{2,1,0:T(8,128)(2,1)}, bf16[64,208,128]{2,1,0:T(8,128)(2,1)S(1)}, u32[]{:S(2)}) copy-start(bf16[64,208,128]{2,1,0:T(8,128)(2,1)S(1)} %all_to_all.10.got_hbm) | copy-start | bytes 10223620
  87.3 11.4 %collective-permute-start = (bf16[256,512]{1,0:T(8,128)(2,1)}, bf16[256,512]{1,0:T(8,128)(2,1)S(1)}, u32[]{:S(2)}, u32[]{:S(2)}) collective-permute-start(bf16[256,512]{1,0:T(8,128)(2,1)} %get-tuple-element.7), channel_id=1, source_target_pairs={{0,32},{16,48},{32,0},{48,16},{1,33},{17,49},{33,1},{49,17},{2,34}... | collective-permute-start | bytes 786440 | tf_op jit(solution)/shard_map/ppermute | solution.py:198
  93.4 18.6 %collective-permute-start.1 = (bf16[256,512]{1,0:T(8,128)(2,1)}, bf16[256,512]{1,0:T(8,128)(2,1)S(1)}, u32[]{:S(2)}, u32[]{:S(2)}) collective-permute-start(bf16[256,512]{1,0:T(8,128)(2,1)} %get-tuple-element.8), channel_id=1, source_target_pairs={{0,16},{16,32},{32,48},{48,0},{1,17},{17,33},{33,49},{49,1},{2,18}... | collective-permute-start | bytes 786440 | tf_op jit(solution)/shard_map/ppermute | solution.py:198
  94.6 23.5 %collective-permute-start.2 = (bf16[256,512]{1,0:T(8,128)(2,1)}, bf16[256,512]{1,0:T(8,128)(2,1)S(1)}, u32[]{:S(2)}, u32[]{:S(2)}) collective-permute-start(bf16[256,512]{1,0:T(8,128)(2,1)} %get-tuple-element.9), channel_id=1, source_target_pairs={{0,48},{16,0},{32,16},{48,32},{1,49},{17,1},{33,17},{49,33},{2,50}... | collective-permute-start | bytes 786440 | tf_op jit(solution)/shard_map/ppermute | solution.py:198
  98.7 19.4 %copy-start.1 = (bf16[256,512]{1,0:T(8,128)(2,1)}, bf16[256,512]{1,0:T(8,128)(2,1)S(1)}, u32[]{:S(2)}) copy-start(bf16[256,512]{1,0:T(8,128)(2,1)S(1)} %collective-permute-done.b_ref) | copy-start | bytes 786436
  112.0 6.1 %copy-start.2 = (bf16[256,512]{1,0:T(8,128)(2,1)}, bf16[256,512]{1,0:T(8,128)(2,1)S(1)}, u32[]{:S(2)}) copy-start(bf16[256,512]{1,0:T(8,128)(2,1)S(1)} %collective-permute-done.1.c_ref) | copy-start | bytes 786436
  118.0 0.7 copy-start.3

commit v2 on v1

v2 whole, which is shorter than its diff:
```python
import functools

import numpy as np
import ml_dtypes
import jax
import jax.numpy as jnp
from jax import lax
from jax.experimental import pallas as pl
from jax.experimental.pallas import tpu as pltpu
from jax.sharding import Mesh, PartitionSpec as P

PIX = 128
SLOTS = 16
HELD = 48
REACH = 10
GROUP = 64
ROWS = 2 * HELD
META = 16
ALL_BLOCKS = GROUP * HELD
TILES = 256
BATCH = 16
STEP = 4
LOADS = 8
PARAMS = pltpu.CompilerParams(vmem_limit_bytes=56 * 2**20)

VMEM_SPEC = pl.BlockSpec(memory_space=pltpu.VMEM)
HBM_SPEC = pl.BlockSpec(memory_space=pltpu.HBM)


def band(spread, degree):
    t = np.arange(-REACH, REACH + 1)
    scaled = t.astype(np.float32) / np.float32(spread)
    taps = np.exp(np.float32(-0.5) * scaled * scaled) * scaled**degree
    taps = (taps / np.sqrt(np.sum(taps * taps))).astype(np.float32)
    out = np.zeros((PIX, PIX), np.float32)
    for k in range(PIX):
        for off, tap in zip(t, taps):
            if 0 <= k + off < PIX:
                out[k, k + off] = tap
    return out


def tables():
    bands = [band(2.0**s, d) for s in range(3) for d in range(3)]
    x_table = np.concatenate([b.T for b in bands], axis=1).astype(ml_dtypes.bfloat16)
    y_table = np.concatenate(bands, axis=1).astype(ml_dtypes.bfloat16)
    return x_table, y_table


def put(staged, i, value):
    for half in range(2):
        staged[pl.ds(half * HELD + i, GROUP, stride=ROWS), :] = value[half * GROUP : (half + 1) * GROUP]


def pack(staged, packed, out_hbm, sems):
    def group(n):
        copies = []
        for half in range(2):
            at = pl.ds(half * HELD + n * BATCH, BATCH)
            for d in range(GROUP):
                row = d * ROWS + half * HELD + n * BATCH
                packed[d, at, :] = staged[row : row + BATCH, :].astype(jnp.bfloat16)
            copies.append(pltpu.make_async_copy(packed.at[:, at, :], out_hbm.at[:, at, :], sems.at[2 * n + half]))
            copies[-1].start()
        return copies

    return group


def weigh_blocks(zh_ref, patch_hbm, slot_hbm, var_hbm, out_hbm, patch_ref, slot_ref, marks, var_ref, staged, packed, in_sems, sems):
    held = HELD // LOADS
    loads = []
    for n in range(LOADS):
        at = pl.ds(n * held, held)
        loads.append(pltpu.make_async_copy(var_hbm.at[at], var_ref.at[at], in_sems.at[n]))
    loads.append(pltpu.make_async_copy(patch_hbm, patch_ref, in_sems.at[LOADS]))
    loads.append(pltpu.make_async_copy(slot_hbm, slot_ref, in_sems.at[LOADS + 1]))
    for c in loads[-2:] + loads[:-2]:
        c.start()
    for c in loads[-2:]:
        c.wait()
    patch, slot = patch_ref[...], slot_ref[...]
    z_at = (patch // 2) % 8
    z_by = (z_at // 2 + 4 - zh_ref[0]) % 4
    owner = ((patch // 16 * 2 + z_at % 2) * 2 + patch % 2) * 4 + slot // 4
    tile = (z_by * 4 + slot % 4) * GROUP + owner
    low = lax.broadcasted_iota(jnp.int32, (META, HELD), 0) < META // 2
    marks[...] = jnp.zeros_like(marks)
    marks[:, :HELD] = jnp.where(low, tile % PIX, tile // PIX).astype(jnp.float32)
    meta = marks[...].astype(jnp.bfloat16)
    for d in range(GROUP):
        packed[d, ROWS:, :] = meta
    rows = pl.ds(ROWS, META)
    copies = [pltpu.make_async_copy(packed.at[:, rows, :], out_hbm.at[:, rows, :], sems.at[6])]
    copies[0].start()
    group = pack(staged, packed, out_hbm, sems)
    for n in range(LOADS):
        loads[n].wait()
        for i in range(n * held, (n + 1) * held):
            put(staged, i, 1.0 / var_ref[i].astype(jnp.float32))
            if i % BATCH == BATCH - 1:
                copies += group(i // BATCH)
    for c in copies:
        c.wait()


def match_blocks(coef_ref, img_ref, var_ref, xt_ref, yt_ref, out_hbm, z_ref, staged, packed, sems):
    step = pl.program_id(0)
    last = pl.num_programs(0) - 1

    cols = lax.broadcasted_iota(jnp.int32, (1, PIX), 1).astype(jnp.float32)
    u = (2.0 * cols - (PIX - 1)) / (PIX - 1)
    rows = lax.broadcasted_iota(jnp.int32, (PIX, 1), 0).astype(jnp.float32)
    v = (2.0 * rows - (PIX - 1)) / (PIX - 1)
    for n in range(STEP):
        base = (step * STEP + n) * 45
        x_all = jnp.dot(img_ref[n], xt_ref[...], preferred_element_type=jnp.float32)

        def flat(b):
            return coef_ref[base + b] + coef_ref[base + 15 + b] * u

        def slope(b):
            return coef_ref[base + 30 + b]

        for s in range(3):
            b = 5 * s
            x0, x1, x2 = (x_all[:, (3 * s + d) * PIX : (3 * s + d + 1) * PIX] for d in range(3))
            parts = (
                (flat(b) * x0 + flat(b + 1) * x1 + flat(b + 3) * x2, slope(b) * x0 + slope(b + 1) * x1 + slope(b + 3) * x2),
                (flat(b + 2) * x0, slope(b + 2) * x0),
                (flat(b + 4) * x0, slope(b + 4) * x0),
            )
            for j in range(3):
                k = (3 * s + j) * PIX
                z_ref[n % 2, k : k + PIX, :PIX] = parts[j][0].astype(jnp.bfloat16)
                z_ref[n % 2, k : k + PIX, PIX:] = parts[j][1].astype(jnp.bfloat16)
        both = jnp.dot(yt_ref[...], z_ref[n % 2], preferred_element_type=jnp.float32)
        matched = both[:, :PIX] + v * both[:, PIX:]
        put(staged, step * STEP + n, matched / var_ref[n].astype(jnp.float32))

    group = pack(staged, packed, out_hbm, sems)
    each = BATCH // STEP
    for n in range(HELD // BATCH):

        @pl.when(step == (n + 1) * each - 1)
        def _():
            group(n)

    @pl.when(step == last)
    def _():
        for n in range(HELD // BATCH):
            for half in range(2):
                at = pl.ds(half * HELD + n * BATCH, BATCH)
                pltpu.make_async_copy(packed.at[:, at, :], out_hbm.at[:, at, :], sems.at[2 * n + half]).wait()


def sum_tiles(halves, id_ref, got_hbm, *refs):
    outs, (blocks, hot, sems) = refs[-3 - len(halves) : -3], refs[-3:]
    held = GROUP // LOADS
    loads = []
    for n in range(LOADS):
        at = pl.ds(n * held, held)
        for half in range(2):
            src = got_hbm.at[at, pl.ds(half * HELD, HELD), :]
            dst = blocks.at[at, :, pl.ds(half * PIX, PIX)]
            loads.append(pltpu.make_async_copy(src, dst, sems.at[2 * n + half]))
    for c in loads:
        c.start()
    tile = lax.broadcasted_iota(jnp.int32, (TILES, PIX), 0)
    for n, (m, out) in enumerate(zip(halves, outs)):
        for k in range(ALL_BLOCKS // PIX):
            ids = id_ref[k : k + 1, :]
            hot[:, k * PIX : (k + 1) * PIX] = jnp.where(ids == tile + m * TILES, 1.0, 0.0).astype(jnp.bfloat16)
        if n == 0:
            for c in loads:
                c.wait()
        values = blocks[...].reshape(ALL_BLOCKS, 2 * PIX)
        out[...] = jnp.dot(hot[...], values, preferred_element_type=jnp.float32).astype(jnp.bfloat16)


def tile_sums(ids, got, halves, after=()):
    part = jax.ShapeDtypeStruct((TILES, 2 * PIX), jnp.bfloat16)
    return pl.pallas_call(
        functools.partial(sum_tiles, halves),
        out_shape=[part] * len(halves),
        in_specs=[VMEM_SPEC, HBM_SPEC] + [pl.BlockSpec(memory_space=pl.ANY)] * len(after),
        out_specs=[VMEM_SPEC] * len(halves),
        scratch_shapes=[
            pltpu.VMEM((GROUP, HELD, 2 * PIX), jnp.bfloat16),
            pltpu.VMEM((TILES, ALL_BLOCKS), jnp.bfloat16),
            pltpu.SemaphoreType.DMA((LOADS * 2,)),
        ],
        compiler_params=PARAMS,
    )(ids, got, *after)


def over_z(part, by):
    return lax.ppermute(part, "zh", [(i, (i + by) % 4) for i in range(4)])


def add_halves(a_ref, b_ref, c_ref, d_ref, out_ref):
    out_ref[...] = sum(ref[...].astype(jnp.float32) for ref in (a_ref, b_ref, c_ref, d_ref))


def add_all(depth_ref, a_ref, b_ref, c_ref, d_ref, out_ref, turned):
    num = sum(ref[...].astype(jnp.float32) for ref in (a_ref, b_ref, c_ref, d_ref))
    for n, total in enumerate((depth_ref[...], num)):
        for half in range(2):
            for s in range(4):
                at = pl.ds((2 * n + half) * 4 + s, GROUP, stride=16)
                turned[at, :] = total[s * GROUP : (s + 1) * GROUP, half * PIX : (half + 1) * PIX]
    out_ref[...] = turned[...].astype(jnp.bfloat16).reshape(GROUP, 16, PIX)


def combine(got_ref, coadd_ref, depth_ref, flat):
    flat[...] = got_ref[...].astype(jnp.float32).reshape(GROUP * 16, PIX)
    for s in range(4):
        for half in range(2):
            rows = slice(half * GROUP, (half + 1) * GROUP)
            depth = flat[pl.ds(half * 4 + s, GROUP, stride=16), :]
            num = flat[pl.ds((2 + half) * 4 + s, GROUP, stride=16), :]
            depth_ref[s, rows, :] = depth
            coadd_ref[s, rows, :] = num / jnp.maximum(depth, 1.0)


def local(images, variance, coefficients, patch_of, slot_of):
    x_table, y_table = tables()
    scratch = [pltpu.VMEM((GROUP * ROWS, PIX), jnp.float32)]
    weight_buf = pl.pallas_call(
        weigh_blocks,
        out_shape=jax.ShapeDtypeStruct((GROUP, ROWS + META, PIX), jnp.bfloat16),
        in_specs=[pl.BlockSpec(memory_space=pltpu.SMEM)] + [HBM_SPEC] * 3,
        out_specs=HBM_SPEC,
        scratch_shapes=[
            pltpu.VMEM((1, HELD), jnp.int32),
            pltpu.VMEM((1, HELD), jnp.int32),
            pltpu.VMEM((META, PIX), jnp.float32),
            pltpu.VMEM((HELD, PIX, PIX), jnp.bfloat16),
        ]
        + scratch
        + [
            pltpu.VMEM((GROUP, ROWS + META, PIX), jnp.bfloat16),
            pltpu.SemaphoreType.DMA((LOADS + 2,)),
            pltpu.SemaphoreType.DMA((7,)),
        ],
        compiler_params=PARAMS,
    )(lax.axis_index("zh").reshape(1), patch_of.reshape(1, HELD), slot_of.reshape(1, HELD), variance)
    group = ("x", "zl", "c", "y")
    weight_got = lax.all_to_all(weight_buf, group, split_axis=0, concat_axis=0, tiled=True)
    matched_buf = pl.pallas_call(
        match_blocks,
        out_shape=jax.ShapeDtypeStruct((GROUP, ROWS, PIX), jnp.bfloat16),
        grid_spec=pltpu.PrefetchScalarGridSpec(
            num_scalar_prefetch=1,
            grid=(HELD // STEP,),
            in_specs=[
                pl.BlockSpec((STEP, PIX, PIX), lambda i, *_: (i, 0, 0)),
                pl.BlockSpec((STEP, PIX, PIX), lambda i, *_: (i, 0, 0)),
                pl.BlockSpec((PIX, 9 * PIX), lambda i, *_: (0, 0)),
                pl.BlockSpec((PIX, 9 * PIX), lambda i, *_: (0, 0)),
            ],
            out_specs=HBM_SPEC,
            scratch_shapes=[pltpu.VMEM((2, 9 * PIX, 2 * PIX), jnp.bfloat16)]
            + scratch
            + [pltpu.VMEM((GROUP, ROWS, PIX), jnp.bfloat16), pltpu.SemaphoreType.DMA((LOADS,))],
        ),
        compiler_params=PARAMS,
        cost_estimate=pl.CostEstimate(flops=6 * 10**9, bytes_accessed=6 * 2**20, transcendentals=0),
    )(coefficients.reshape(-1), images, variance, jnp.asarray(x_table), jnp.asarray(y_table))
    matched_got = lax.all_to_all(matched_buf, group, split_axis=0, concat_axis=0, tiled=True)
    code = weight_got[:, ROWS :: META // 2, :HELD].astype(jnp.int32)
    ids = (code[:, 0] + PIX * code[:, 1]).reshape(ALL_BLOCKS // PIX, PIX)
    weight_parts = tile_sums(ids, weight_got, (0, 1, 2, 3))
    depth = pl.pallas_call(
        add_halves,
        out_shape=jax.ShapeDtypeStruct((TILES, 2 * PIX), jnp.float32),
        in_specs=[VMEM_SPEC] * 4,
        out_specs=VMEM_SPEC,
        compiler_params=PARAMS,
    )(weight_parts[0], *(over_z(weight_parts[by], by) for by in (2, 1, 3)))
    own, up, far, down = tile_sums(ids, matched_got, (0, 1, 2, 3), (weight_parts[0],))
    summed = pl.pallas_call(
        add_all,
        out_shape=jax.ShapeDtypeStruct((GROUP, 16, PIX), jnp.bfloat16),
        in_specs=[VMEM_SPEC] * 5,
        out_specs=VMEM_SPEC,
        scratch_shapes=[pltpu.VMEM((GROUP * 16, PIX), jnp.float32)],
        compiler_params=PARAMS,
    )(depth, own, over_z(far, 2), over_z(up, 1), over_z(down, 3))
    whole = lax.all_to_all(summed, group, split_axis=0, concat_axis=0, tiled=True)
    out = jax.ShapeDtypeStruct((4, PIX, PIX), jnp.float32)
    return pl.pallas_call(
        combine,
        out_shape=(out, out),
        in_specs=[VMEM_SPEC],
        out_specs=(VMEM_SPEC, VMEM_SPEC),
        scratch_shapes=[pltpu.VMEM((GROUP * 16, PIX), jnp.float32)],
        compiler_params=PARAMS,
    )(whole)


def solution(mesh):
    names = ("x", "zh", "zl", "c", "y")
    fine = Mesh(mesh.devices.reshape(4, 4, 2, 2, 4), names)
    return jax.shard_map(
        local,
        mesh=fine,
        in_specs=(P(names, None, None), P(names, None, None), P(names, None, None), P(names, None), P(names)),
        out_specs=(P(names, None, None), P(names, None, None)),
        check_vma=False,
    )
```

time: 138 us -> 119 us (0.86)
  blocking collectives: 67.4 us -> 16.4 us
  starting transfers between devices: 9.68 us -> 35.9 us
  Pallas kernels: 33.2 us -> 41.3 us
  waiting for transfers between devices: 21.1 us -> 17.4 us
    all_to_all x1 -> x0, blocking collectives: 52.5 us -> none  [local(): got = lax.all_to_all(buf, group, split_axis=0, concat_axis=0, tiled=True)]
    all_to_all x0 -> x2, starting transfers between devices: none -> 16.1 us  [the longest x1 10.4 us: local(): lax.all_to_all(weight_buf, group, split_axis=0, concat_axis=0, tiled=True)]
    ppermute x3 -> x6, waiting for transfers between devices: 21.1 us -> 5.25 us  [over_z(): return lax.ppermute(part, 'zh', [(i, (i + by) % 4) for i in range(4)])]
    all_to_all x0 -> x2, waiting for transfers between devices: none -> 12.1 us  [the longest x1 7.94 us: local(): lax.all_to_all(matched_buf, group, split_axis=0, concat_axis=0, tiled=True)]
    ppermute x3 -> x6, starting transfers between devices: 9.68 us -> 19.8 us  [over_z(): return lax.ppermute(part, 'zh', [(i, (i + by) % 4) for i in range(4)])]
    pallas_call x3 -> x6, Pallas kernels: 31.3 us -> 39.3 us  [the longest x1 19.8 us: local(): pl.pallas_call(match_blocks, out_shape=jax.ShapeDtypeStruct((GROUP, ROWS,...]
    unnamed x9 -> x19, local copies, waits for them, and re-layouts: 1.55 us -> 3.33 us
    all_to_all x1, blocking collectives: 14.9 us -> 16.4 us  [local(): lax.all_to_all(summed, group, split_axis=0, concat_axis=0, tiled=True)]
  transfers between devices with their start and end apart: 3 -> 8, of which waited for: 3 -> 3; matrix products, arithmetic and copies ran while one was open for 0% -> 2% of each run, Pallas kernels for 0% -> 27%
where the time goes in v2:
time: 119 us; the launch traced here: 118 us
  Pallas kernels  41.3 us (35%)
  starting transfers between devices  35.9 us (30%)
  waiting for transfers between devices  17.4 us (15%)
  blocking collectives  16.4 us (14%)
  local copies, waits for them, and re-layouts  5.95 us (5%)
    ppermute x6, starting transfers between devices, over_z(): return lax.ppermute(part, 'zh', [(i, (i + by) % 4) for i in range(4)])  19.8 us
    pallas_call x1, Pallas kernels, local(): pl.pallas_call(match_blocks, out_shape=jax.ShapeDtypeStruct((GROUP, ROWS,...  19.8 us
    all_to_all x1, blocking collectives, local(): lax.all_to_all(summed, group, split_axis=0, concat_axis=0, tiled=True)  16.4 us
    all_to_all x1, starting transfers between devices, local(): lax.all_to_all(weight_buf, group, split_axis=0, concat_axis=0, tiled=True)  10.4 us
    pallas_call x2, Pallas kernels, tile_sums(): pl.pallas_call(functools.partial(sum_tiles, halves), out_shape=[part] * l...  10.3 us
    all_to_all x1, waiting for transfers between devices, local(): lax.all_to_all(matched_buf, group, split_axis=0, concat_axis=0, tiled=True)  7.94 us
    all_to_all x1, starting transfers between devices, local(): lax.all_to_all(matched_buf, group, split_axis=0, concat_axis=0, tiled=True)  5.75 us
    ppermute x6, waiting for transfers between devices, over_z(): return lax.ppermute(part, 'zh', [(i, (i + by) % 4) for i in range(4)])  5.25 us
  transfers between devices with their start and end apart: 8, of which 3 were waited for; matrix products, arithmetic and copies ran while one was open for 2% of the time, Pallas kernels for 27%

profile of v2, /device:TPU:1, one launch (start us, length us, event | category | flops | bytes accessed | tf_op | source)
XLA Modules:
  0.0 117.8 jit_solution(3585438071454624045)
XLA Ops:
  0.6 5.2 %shard_map.86 = bf16[64,112,128]{2,1,0:T(8,128)(2,1)} custom-call(s32[1]{0:T(128)} %bitcast.zh_ref, s32[1,48]{1,0:T(1,128)} %bitcast.3, s32[1,48]{1,0:T(1,128)} %bitcast.4, bf16[48,128,128]{2,1,0:T(8,128)(2,1)} %var_ref.1), custom_call_target="tpu_custom_call" | custom-call | tf_op jit(solution)/shard_map/pallas_call | solution.py:229
  5.9 0.0 copy-start.8
  5.9 10.4 %all-to-all-start = ((bf16[64,112,128]{2,1,0:T(8,128)(2,1)}), bf16[64,112,128]{2,1,0:T(8,128)(2,1)S(1)}, u32[]{:S(2)}, u32[]{:S(2)}) async-start(bf16[64,112,128]{2,1,0:T(8,128)(2,1)} %shard_map.86), calls=%async_computation | async-start | bytes 3670016 | tf_op jit(solution)/shard_map/all_to_all | solution.py:249
  16.3 0.0 copy-done.8
  16.3 0.1 copy.9
  16.4 0.8 reshape.25.coef_ref
  17.2 19.8 %shard_map.89 = bf16[64,96,128]{2,1,0:T(8,128)(2,1)} custom-call(f32[2160]{0:T(1024)} %reshape.25.coef_ref, bf16[48,128,128]{2,1,0:T(8,128)(2,1)} %img_ref.1, bf16[48,128,128]{2,1,0:T(8,128)(2,1)} %var_ref.1, bf16[128,1152]{1,0:T(8,128)(2,1)} %constant.12.clone.xt_ref, bf16[128,1152]{1,0:T(8,128)(2,1)} %constant.13.clone.yt_ref), custom_call_target="tpu_custom_call" | custom-call | flops 6000000000 | bytes 6291456 | tf_op jit(solution)/shard_map/pallas_call | solution.py:250
  37.0 4.2 %all-to-all-done.got_hbm = bf16[64,112,128]{2,1,0:T(8,128)(2,1)S(1)} async-done(((bf16[64,112,128]{2,1,0:T(8,128)(2,1)}), bf16[64,112,128]{2,1,0:T(8,128)(2,1)S(1)}, u32[]{:S(2)}, u32[]{:S(2)}) %all-to-all-start) | async-done | bytes 1835040 | tf_op jit(solution)/shard_map/all_to_all | solution.py:249
  41.2 0.0 copy-start
  41.2 5.8 %all-to-all-start.1 = ((bf16[64,96,128]{2,1,0:T(8,128)(2,1)}), bf16[64,96,128]{2,1,0:T(8,128)(2,1)S(1)}, u32[]{:S(2)}, u32[]{:S(2)}) async-start(bf16[64,96,128]{2,1,0:T(8,128)(2,1)} %shard_map.89), calls=%async_computation.1 | async-start | bytes 3145728 | tf_op jit(solution)/shard_map/all_to_all | solution.py:270
  47.0 0.0 copy-done
  47.0 1.1 slice.9
  48.2 0.1 fusion.1
  48.3 0.7 add.8.id_ref
  49.0 5.2 %shard_map.87 = (bf16[256,256]{1,0:T(8,128)(2,1)}, bf16[256,256]{1,0:T(8,128)(2,1)}, bf16[256,256]{1,0:T(8,128)(2,1)}, bf16[256,256]{1,0:T(8,128)(2,1)}) custom-call(s32[24,128]{1,0:T(8,128)} %add.8.id_ref, bf16[64,112,128]{2,1,0:T(8,128)(2,1)} %copy-done), custom_call_target="tpu_custom_call" | custom-call | tf_op jit(solution)/shard_map/pallas_call | solution.py:183
  54.1 6.1 %collective-permute-start = (bf16[256,256]{1,0:T(8,128)(2,1)}, bf16[256,256]{1,0:T(8,128)(2,1)S(1)}, u32[]{:S(2)}, u32[]{:S(2)}) collective-permute-start(bf16[256,256]{1,0:T(8,128)(2,1)} %get-tuple-element.11), channel_id=1, source_target_pairs={{0,32},{16,48},{32,0},{48,16},{1,33},{17,49},{33,1},{49,17},{2,34}... | collective-permute-start | bytes 393224 | tf_op jit(solution)/shard_map/ppermute | solution.py:198
  60.2 1.2 %collective-permute-start.1 = (bf16[256,256]{1,0:T(8,128)(2,1)}, bf16[256,256]{1,0:T(8,128)(2,1)S(1)}, u32[]{:S(2)}, u32[]{:S(2)}) collective-permute-start(bf16[256,256]{1,0:T(8,128)(2,1)} %get-tuple-element.12), channel_id=1, source_target_pairs={{0,16},{16,32},{32,48},{48,0},{1,17},{17,33},{33,49},{49,1},{2,18}... | collective-permute-start | bytes 393224 | tf_op jit(solution)/shard_map/ppermute | solution.py:198
  61.4 2.4 %collective-permute-start.2 = (bf16[256,256]{1,0:T(8,128)(2,1)}, bf16[256,256]{1,0:T(8,128)(2,1)S(1)}, u32[]{:S(2)}, u32[]{:S(2)}) collective-permute-start(bf16[256,256]{1,0:T(8,128)(2,1)} %get-tuple-element.13), channel_id=1, source_target_pairs={{0,48},{16,0},{32,16},{48,32},{1,49},{17,1},{33,17},{49,33},{2,50}... | collective-permute-start | bytes 393224 | tf_op jit(solution)/shard_map/ppermute | solution.py:198
  63.8 7.9 %all-to-all-done.1.got_hbm = bf16[64,96,128]{2,1,0:T(8,128)(2,1)S(1)} async-done(((bf16[64,96,128]{2,1,0:T(8,128)(2,1)}), bf16[64,96,128]{2,1,0:T(8,128)(2,1)S(1)}, u32[]{:S(2)}, u32[]{:S(2)}) %all-to-all-start.1) | async-done | bytes 1572896 | tf_op jit(solution)/shard_map/all_to_all | solution.py:270
  71.7 0.0 copy-start.1
  71.7 1.2 copy-done.1
  72.9 5.2 %shard_map.90 = (bf16[256,256]{1,0:T(8,128)(2,1)}, bf16[256,256]{1,0:T(8,128)(2,1)}, bf16[256,256]{1,0:T(8,128)(2,1)}, bf16[256,256]{1,0:T(8,128)(2,1)}) custom-call(s32[24,128]{1,0:T(8,128)} %add.8.id_ref, bf16[64,96,128]{2,1,0:T(8,128)(2,1)} %copy-done.1, bf16[256,256]{1,0:T(8,128)(2,1)} %get-tuple-element.10.a_ref.refs_0_), custom_call_target="tpu_custom_call" | custom-call | tf_op jit(solution)/shard_map/pallas_call | solution.py:183
  78.1 6.5 %collective-permute-start.3 = (bf16[256,256]{1,0:T(8,128)(2,1)}, bf16[256,256]{1,0:T(8,128)(2,1)S(1)}, u32[]{:S(2)}, u32[]{:S(2)}) collective-permute-start(bf16[256,256]{1,0:T(8,128)(2,1)} %get-tuple-element.15), channel_id=1, source_target_pairs={{0,32},{16,48},{32,0},{48,16},{1,33},{17,49},{33,1},{49,17},{2,34}... | collective-permute-start | bytes 393224 | tf_op jit(solution)/shard_map/ppermute | solution.py:198
  84.6 3.6 %collective-permute-start.4 = (bf16[256,256]{1,0:T(8,128)(2,1)}, bf16[256,256]{1,0:T(8,128)(2,1)S(1)}, u32[]{:S(2)}, u32[]{:S(2)}) collective-permute-start(bf16[256,256]{1,0:T(8,128)(2,1)} %get-tuple-element.16), channel_id=1, source_target_pairs={{0,16},{16,32},{32,48},{48,0},{1,17},{17,33},{33,49},{49,1},{2,18}... | collective-permute-start | bytes 393224 | tf_op jit(solution)/shard_map/ppermute | solution.py:198
  88.2 0.0 collective-permute-done.b_ref
  88.2 0.0 copy-start.2
  88.2 0.0 collective-permute-start.5
  88.2 0.0 collective-permute-done.1.c_ref
  88.2 0.0 copy-start.3
  88.2 0.0 collective-permute-done.2.d_ref
  88.2 0.6 copy-done.2
  88.9 0.1 copy-done.3
  88.9 0.0 copy-start.4
  88.9 0.7 copy-done.4
  89.6 1.9 %shard_map.88.depth_ref = f32[256,256]{1,0:T(8,128)} custom-call(bf16[256,256]{1,0:T(8,128)(2,1)} %get-tuple-element.10.a_ref.refs_0_, bf16[256,256]{1,0:T(8,128)(2,1)} %copy-done.2, bf16[256,256]{1,0:T(8,128)(2,1)} %copy-done.3, bf16[256,256]{1,0:T(8,128)(2,1)} %copy-done.4), custom_call_target="tpu_custom_call" | custom-call | tf_op jit(solution)/shard_map/pallas_call | solution.py:274
  91.4 0.0 collective-permute-done.3.b_ref
  91.4 0.0 copy-start.5
  91.4 5.2 %collective-permute-done.4.c_ref = bf16[256,256]{1,0:T(8,128)(2,1)S(1)} collective-permute-done((bf16[256,256]{1,0:T(8,128)(2,1)}, bf16[256,256]{1,0:T(8,128)(2,1)S(1)}, u32[]{:S(2)}, u32[]{:S(2)}) %collective-permute-start.4) | collective-permute-done | bytes 131104 | tf_op jit(solution)/shard_map/ppermute | solution.py:198
  96.7 0.0 copy-start.6
  96.7 0.0 collective-permute-done.5.d_ref
  96.7 0.0 copy-start.7
  96.7 0.0 copy-done.5
  96.7 0.6 copy-done.6
  97.3 0.0 copy-done.7
  97.4 2.1 %shard_map.91 = bf16[64,16,128]{2,1,0:T(8,128)(2,1)} custom-call(f32[256,256]{1,0:T(8,128)} %shard_map.88.depth_ref, bf16[256,256]{1,0:T(8,128)(2,1)} %get-tuple-element.14.a_ref, bf16[256,256]{1,0:T(8,128)(2,1)} %copy-done.5, bf16[256,256]{1,0:T(8,128)(2,1)} %copy-done.6, bf16[256,256]{1,0:T(8,128)(2,1)} %copy-done.7), custom_call_target="tpu_custom_call" | custom-call | tf_op jit(solution)/shard_map/pallas_call | solution.py:282
  99.5 16.4 %all_to_all.15.got_ref = bf16[64,16,128]{2,1,0:T(8,128)(2,1)} all-to-all(bf16[64,16,128]{2,1,0:T(8,128)(2,1)} %shard_map.91), channel_id=1, replica_groups=mesh['x'=4,'zh'=4,'zl'=2,'c'=2,'y'=4] {'x','zl','c','y'}, dimensions={0} | all-to-all | bytes 524288 | tf_op jit(solution)/shard_map/all_to_all | solution.py:290
  115.9 1.9 %shard_map.92 = (f32[4,128,128]{2,1,0:T(8,128)}, f32[4,128,128]{2,1,0:T(8,128)}) custom-call(bf16[64,16,128]{2,1,0:T(8,128)(2,1)} %all_to_all.15.got_ref), custom_call_target="tpu_custom_call" | custom-call | tf_op jit(solution)/shard_map/pallas_call | solution.py:292
  (1 shorter events, 0.0 us)
Async XLA Ops:
  5.9 10.4 %copy-start.8 = (f32[48,3,15]{0,2,1:T(8,128)S(1)}, f32[48,3,15]{0,2,1:T(8,128)}, u32[]{:S(2)}) copy-start(f32[48,3,15]{0,2,1:T(8,128)} %param.9) | copy-start | bytes 25924
  5.9 35.3 %all-to-all-start = ((bf16[64,112,128]{2,1,0:T(8,128)(2,1)}), bf16[64,112,128]{2,1,0:T(8,128)(2,1)S(1)}, u32[]{:S(2)}, u32[]{:S(2)}) async-start(bf16[64,112,128]{2,1,0:T(8,128)(2,1)} %shard_map.86), calls=%async_computation | async-start | bytes 3670016 | tf_op jit(solution)/shard_map/all_to_all | solution.py:249
  41.2 5.8 %copy-start = (bf16[64,112,128]{2,1,0:T(8,128)(2,1)}, bf16[64,112,128]{2,1,0:T(8,128)(2,1)S(1)}, u32[]{:S(2)}) copy-start(bf16[64,112,128]{2,1,0:T(8,128)(2,1)S(1)} %all-to-all-done.got_hbm) | copy-start | bytes 5505028
  41.2 30.5 %all-to-all-start.1 = ((bf16[64,96,128]{2,1,0:T(8,128)(2,1)}), bf16[64,96,128]{2,1,0:T(8,128)(2,1)S(1)}, u32[]{:S(2)}, u32[]{:S(2)}) async-start(bf16[64,96,128]{2,1,0:T(8,128)(2,1)} %shard_map.89), calls=%async_computation.1 | async-start | bytes 3145728 | tf_op jit(solution)/shard_map/all_to_all | solution.py:270
  54.1 34.1 %collective-permute-start = (bf16[256,256]{1,0:T(8,128)(2,1)}, bf16[256,256]{1,0:T(8,128)(2,1)S(1)}, u32[]{:S(2)}, u32[]{:S(2)}) collective-permute-start(bf16[256,256]{1,0:T(8,128)(2,1)} %get-tuple-element.11), channel_id=1, source_target_pairs={{0,32},{16,48},{32,0},{48,16},{1,33},{17,49},{33,1},{49,17},{2,34}... | collective-permute-start | bytes 393224 | tf_op jit(solution)/shard_map/ppermute | solution.py:198
  60.2 28.0 %collective-permute-start.1 = (bf16[256,256]{1,0:T(8,128)(2,1)}, bf16[256,256]{1,0:T(8,128)(2,1)S(1)}, u32[]{:S(2)}, u32[]{:S(2)}) collective-permute-start(bf16[256,256]{1,0:T(8,128)(2,1)} %get-tuple-element.12), channel_id=1, source_target_pairs={{0,16},{16,32},{32,48},{48,0},{1,17},{17,33},{33,49},{49,1},{2,18}... | collective-permute-start | bytes 393224 | tf_op jit(solution)/shard_map/ppermute | solution.py:198
  61.4 26.8 %collective-permute-start.2 = (bf16[256,256]{1,0:T(8,128)(2,1)}, bf16[256,256]{1,0:T(8,128)(2,1)S(1)}, u32[]{:S(2)}, u32[]{:S(2)}) collective-permute-start(bf16[256,256]{1,0:T(8,128)(2,1)} %get-tuple-element.13), channel_id=1, source_target_pairs={{0,48},{16,0},{32,16},{48,32},{1,49},{17,1},{33,17},{49,33},{2,50}... | collective-permute-start | bytes 393224 | tf_op jit(solution)/shard_map/ppermute | solution.py:198
  71.7 1.2 copy-start.1
  78.1 13.4 %collective-permute-start.3 = (bf16[256,256]{1,0:T(8,128)(2,1)}, bf16[256,256]{1,0:T(8,128)(2,1)S(1)}, u32[]{:S(2)}, u32[]{:S(2)}) collective-permute-start(bf16[256,256]{1,0:T(8,128)(2,1)} %get-tuple-element.15), channel_id=1, source_target_pairs={{0,32},{16,48},{32,0},{48,16},{1,33},{17,49},{33,1},{49,17},{2,34}... | collective-permute-start | bytes 393224 | tf_op jit(solution)/shard_map/ppermute | solution.py:198
  84.6 12.1 %collective-permute-start.4 = (bf16[256,256]{1,0:T(8,128)(2,1)}, bf16[256,256]{1,0:T(8,128)(2,1)S(1)}, u32[]{:S(2)}, u32[]{:S(2)}) collective-permute-start(bf16[256,256]{1,0:T(8,128)(2,1)} %get-tuple-element.16), channel_id=1, source_target_pairs={{0,16},{16,32},{32,48},{48,0},{1,17},{17,33},{33,49},{49,1},{2,18}... | collective-permute-start | bytes 393224 | tf_op jit(solution)/shard_map/ppermute | solution.py:198
  88.2 0.7 copy-start.2
  88.2 8.5 %collective-permute-start.5 = (bf16[256,256]{1,0:T(8,128)(2,1)}, bf16[256,256]{1,0:T(8,128)(2,1)S(1)}, u32[]{:S(2)}, u32[]{:S(2)}) collective-permute-start(bf16[256,256]{1,0:T(8,128)(2,1)} %get-tuple-element.17), channel_id=1, source_target_pairs={{0,48},{16,0},{32,16},{48,32},{1,49},{17,1},{33,17},{49,33},{2,50}... | collective-permute-start | bytes 393224 | tf_op jit(solution)/shard_map/ppermute | solution.py:198
  88.2 0.7 copy-start.3
  88.9 0.7 copy-start.4
  91.4 5.3 %copy-start.5 = (bf16[256,256]{1,0:T(8,128)(2,1)}, bf16[256,256]{1,0:T(8,128)(2,1)S(1)}, u32[]{:S(2)}) copy-start(bf16[256,256]{1,0:T(8,128)(2,1)S(1)} %collective-permute-done.3.b_ref) | copy-start | bytes 393220
  96.7 0.7 copy-start.6
  96.7 0.7 copy-start.7

commit v3 on v2

--- a/solution.py
+++ b/solution.py
@@ -22,9 +22,12 @@
 STEP = 4
 LOADS = 8
 PARAMS = pltpu.CompilerParams(vmem_limit_bytes=56 * 2**20)
+SUM_PARAMS = pltpu.CompilerParams(vmem_limit_bytes=24 * 2**20)
+ADD_PARAMS = pltpu.CompilerParams(vmem_limit_bytes=8 * 2**20)
 
 VMEM_SPEC = pl.BlockSpec(memory_space=pltpu.VMEM)
 HBM_SPEC = pl.BlockSpec(memory_space=pltpu.HBM)
+ANY_SPEC = pl.BlockSpec(memory_space=pl.ANY)
 
 
 def band(spread, degree):
@@ -97,7 +100,7 @@
     for n in range(LOADS):
         loads[n].wait()
         for i in range(n * held, (n + 1) * held):
-            put(staged, i, 1.0 / var_ref[i].astype(jnp.float32))
+            put(staged, i, pl.reciprocal(var_ref[i].astype(jnp.float32), approx=True))
             if i % BATCH == BATCH - 1:
                 copies += group(i // BATCH)
     for c in copies:
@@ -154,44 +157,61 @@
                 pltpu.make_async_copy(packed.at[:, at, :], out_hbm.at[:, at, :], sems.at[2 * n + half]).wait()
 
 
-def sum_tiles(halves, id_ref, got_hbm, *refs):
-    outs, (blocks, hot, sems) = refs[-3 - len(halves) : -3], refs[-3:]
-    held = GROUP // LOADS
-    loads = []
-    for n in range(LOADS):
-        at = pl.ds(n * held, held)
-        for half in range(2):
-            src = got_hbm.at[at, pl.ds(half * HELD, HELD), :]
-            dst = blocks.at[at, :, pl.ds(half * PIX, PIX)]
-            loads.append(pltpu.make_async_copy(src, dst, sems.at[2 * n + half]))
-    for c in loads:
-        c.start()
-    tile = lax.broadcasted_iota(jnp.int32, (TILES, PIX), 0)
-    for n, (m, out) in enumerate(zip(halves, outs)):
-        for k in range(ALL_BLOCKS // PIX):
-            ids = id_ref[k : k + 1, :]
-            hot[:, k * PIX : (k + 1) * PIX] = jnp.where(ids == tile + m * TILES, 1.0, 0.0).astype(jnp.bfloat16)
-        if n == 0:
-            for c in loads:
-                c.wait()
-        values = blocks[...].reshape(ALL_BLOCKS, 2 * PIX)
-        out[...] = jnp.dot(hot[...], values, preferred_element_type=jnp.float32).astype(jnp.bfloat16)
-
-
-def tile_sums(ids, got, halves, after=()):
+def read_marks(got_ref, table, id_ref):
+    code = got_ref[:, ROWS:, :].astype(jnp.float32)
+    lane = lax.broadcasted_iota(jnp.int32, (GROUP, PIX), 1)
+    tile = code[:, 0, :] + PIX * code[:, META // 2, :]
+    table[...] = jnp.where(lane < HELD, tile, 0.0).astype(jnp.int32)
+    lane = lax.broadcasted_iota(jnp.int32, (8, PIX), 1)
+    rows = [jnp.zeros((8, PIX), jnp.int32)] * 4
+    for n in range(8):
+        row, at = n * HELD // PIX, n * HELD % PIX
+        moved = pltpu.roll(table[pl.ds(n, 8, stride=8), :], at, 1) if at else table[pl.ds(n, 8, stride=8), :]
+        rows[row] = rows[row] + jnp.where(lane >= at, moved, 0)
+        rows[row + 1] = rows[row + 1] + jnp.where(lane < at, moved, 0)
+    for row in range(3):
+        id_ref[pl.ds(row, 8, stride=3), :] = rows[row]
+
+
+def sum_blocks(id_ref, got_ref, outs, hot):
+    tile = lax.broadcasted_iota(jnp.int32, (4 * TILES, PIX), 0)
+    for k in range(ALL_BLOCKS // PIX):
+        hot[:, k * PIX : (k + 1) * PIX] = jnp.where(id_ref[k : k + 1, :] == tile, 1.0, 0.0).astype(jnp.bfloat16)
+    halves = [got_ref[:, half * HELD : (half + 1) * HELD, :].reshape(ALL_BLOCKS, PIX) for half in range(2)]
+    total = jnp.dot(hot[...], jnp.concatenate(halves, axis=1), preferred_element_type=jnp.float32).astype(jnp.bfloat16)
+    for m, out in enumerate(outs):
+        out[...] = total[m * TILES : (m + 1) * TILES]
+
+
+def sum_weights(got_ref, id_ref, *refs):
+    read_marks(got_ref, refs[5], id_ref)
+    sum_blocks(id_ref, got_ref, refs[:4], refs[4])
+
+
+def sum_matched(id_ref, got_ref, *refs):
+    sum_blocks(id_ref, got_ref, refs[:4], refs[4])
+
+
+def tile_sums(got, ids=None):
     part = jax.ShapeDtypeStruct((TILES, 2 * PIX), jnp.bfloat16)
+    hot = pltpu.VMEM((4 * TILES, ALL_BLOCKS), jnp.bfloat16)
+    if ids is not None:
+        return pl.pallas_call(
+            sum_matched,
+            out_shape=[part] * 4,
+            in_specs=[VMEM_SPEC] * 2,
+            out_specs=[VMEM_SPEC] * 4,
+            scratch_shapes=[hot],
+            compiler_params=SUM_PARAMS,
+        )(ids, got)
     return pl.pallas_call(
-        functools.partial(sum_tiles, halves),
-        out_shape=[part] * len(halves),
-        in_specs=[VMEM_SPEC, HBM_SPEC] + [pl.BlockSpec(memory_space=pl.ANY)] * len(after),
-        out_specs=[VMEM_SPEC] * len(halves),
-        scratch_shapes=[
-            pltpu.VMEM((GROUP, HELD, 2 * PIX), jnp.bfloat16),
-            pltpu.VMEM((TILES, ALL_BLOCKS), jnp.bfloat16),
-            pltpu.SemaphoreType.DMA((LOADS * 2,)),
-        ],
-        compiler_params=PARAMS,
-    )(ids, got, *after)
+        sum_weights,
+        out_shape=[jax.ShapeDtypeStruct((ALL_BLOCKS // PIX, PIX), jnp.int32)] + [part] * 4,
+        in_specs=[VMEM_SPEC],
+        out_specs=[VMEM_SPEC] * 5,
+        scratch_shapes=[hot, pltpu.VMEM((GROUP, PIX), jnp.int32)],
+        compiler_params=SUM_PARAMS,
+    )(got)
 
 
 def over_z(part, by):
@@ -268,24 +288,22 @@
         cost_estimate=pl.CostEstimate(flops=6 * 10**9, bytes_accessed=6 * 2**20, transcendentals=0),
     )(coefficients.reshape(-1), images, variance, jnp.asarray(x_table), jnp.asarray(y_table))
     matched_got = lax.all_to_all(matched_buf, group, split_axis=0, concat_axis=0, tiled=True)
-    code = weight_got[:, ROWS :: META // 2, :HELD].astype(jnp.int32)
-    ids = (code[:, 0] + PIX * code[:, 1]).reshape(ALL_BLOCKS // PIX, PIX)
-    weight_parts = tile_sums(ids, weight_got, (0, 1, 2, 3))
+    ids, *weight_parts = tile_sums(weight_got)
     depth = pl.pallas_call(
         add_halves,
         out_shape=jax.ShapeDtypeStruct((TILES, 2 * PIX), jnp.float32),
         in_specs=[VMEM_SPEC] * 4,
         out_specs=VMEM_SPEC,
-        compiler_params=PARAMS,
+        compiler_params=ADD_PARAMS,
     )(weight_parts[0], *(over_z(weight_parts[by], by) for by in (2, 1, 3)))
-    own, up, far, down = tile_sums(ids, matched_got, (0, 1, 2, 3), (weight_parts[0],))
+    own, up, far, down = tile_sums(matched_got, ids)
     summed = pl.pallas_call(
         add_all,
         out_shape=jax.ShapeDtypeStruct((GROUP, 16, PIX), jnp.bfloat16),
         in_specs=[VMEM_SPEC] * 5,
         out_specs=VMEM_SPEC,
         scratch_shapes=[pltpu.VMEM((GROUP * 16, PIX), jnp.float32)],
-        compiler_params=PARAMS,
+        compiler_params=ADD_PARAMS,
     )(depth, own, over_z(far, 2), over_z(up, 1), over_z(down, 3))
     whole = lax.all_to_all(summed, group, split_axis=0, concat_axis=0, tiled=True)
     out = jax.ShapeDtypeStruct((4, PIX, PIX), jnp.float32)
@@ -295,7 +313,7 @@
         in_specs=[VMEM_SPEC],
         out_specs=(VMEM_SPEC, VMEM_SPEC),
         scratch_shapes=[pltpu.VMEM((GROUP * 16, PIX), jnp.float32)],
-        compiler_params=PARAMS,
+        compiler_params=ADD_PARAMS,
     )(whole)
 
 

time: 119 us -> 112 us (0.941)
  Pallas kernels: 41.3 us -> 31.2 us
  waiting for transfers between devices: 17.4 us -> 26.9 us
  local copies, waits for them, and re-layouts: 5.95 us -> 0.93 us
    pallas_call x2, Pallas kernels: 10.3 us -> 4.86 us  [the longest x1 2.87 us: tile_sums(): pl.pallas_call(sum_weights, out_shape=[jax.ShapeDtypeStruct((ALL_BLOCKS /...]
    all_to_all x1, waiting for transfers between devices: 7.94 us -> 12.7 us  [local(): lax.all_to_all(matched_buf, group, split_axis=0, concat_axis=0, tiled=True)]
    ppermute x6, waiting for transfers between devices: 5.25 us -> 10 us  [over_z(): return lax.ppermute(part, 'zh', [(i, (i + by) % 4) for i in range(4)])]
    unnamed x19 -> x3, local copies, waits for them, and re-layouts: 3.33 us -> 0.12 us
    pallas_call x1, Pallas kernels: 2.12 us -> 0.26 us  [local(): pl.pallas_call(add_all, out_shape=jax.ShapeDtypeStruct((GROUP, 16, PIX),...]
    pallas_call x1, Pallas kernels: 1.86 us -> 0.07 us  [local(): pl.pallas_call(add_halves, out_shape=jax.ShapeDtypeStruct((TILES, 2 * PIX...]
  transfers between devices with their start and end apart: 8 -> 8, of which waited for: 3 -> 4; matrix products, arithmetic and copies ran while one was open for 2% -> 1% of each run, Pallas kernels for 27% -> 22%
where the time goes in v3:
time: 112 us
  starting transfers between devices  35.4 us (32%)
  Pallas kernels  31.2 us (28%)
  waiting for transfers between devices  26.9 us (24%)
  blocking collectives  16.5 us (15%)
    pallas_call x1, Pallas kernels, local(): pl.pallas_call(match_blocks, out_shape=jax.ShapeDtypeStruct((GROUP, ROWS,...  19.8 us
    ppermute x6, starting transfers between devices, over_z(): return lax.ppermute(part, 'zh', [(i, (i + by) % 4) for i in range(4)])  19.3 us
    all_to_all x1, blocking collectives, local(): lax.all_to_all(summed, group, split_axis=0, concat_axis=0, tiled=True)  16.5 us
    all_to_all x1, waiting for transfers between devices, local(): lax.all_to_all(matched_buf, group, split_axis=0, concat_axis=0, tiled=True)  12.7 us
    all_to_all x1, starting transfers between devices, local(): lax.all_to_all(weight_buf, group, split_axis=0, concat_axis=0, tiled=True)  10.4 us
    ppermute x6, waiting for transfers between devices, over_z(): return lax.ppermute(part, 'zh', [(i, (i + by) % 4) for i in range(4)])  10 us
    all_to_all x1, starting transfers between devices, local(): lax.all_to_all(matched_buf, group, split_axis=0, concat_axis=0, tiled=True)  5.75 us
    pallas_call x1, Pallas kernels, local(): pl.pallas_call(weigh_blocks, out_shape=jax.ShapeDtypeStruct((GROUP, ROWS...  5.2 us
  transfers between devices with their start and end apart: 8, of which 4 were waited for; matrix products, arithmetic and copies ran while one was open for 1% of the time, Pallas kernels for 22%

profile of v3, /device:TPU:1, one launch (start us, length us, event | category | flops | bytes accessed | tf_op | source)
XLA Modules:
  0.0 111.7 jit_solution(2093529054303743848)
XLA Ops:
  0.6 5.2 %shard_map.86 = bf16[64,112,128]{2,1,0:T(8,128)(2,1)} custom-call(s32[1]{0:T(128)} %bitcast.zh_ref, s32[1,48]{1,0:T(1,128)} %bitcast.3, s32[1,48]{1,0:T(1,128)} %bitcast.4, bf16[48,128,128]{2,1,0:T(8,128)(2,1)} %var_ref.1), custom_call_target="tpu_custom_call" | custom-call | tf_op jit(solution)/shard_map/pallas_call | solution.py:249
  5.8 0.0 copy-start
  5.9 10.4 %all-to-all-start = ((bf16[64,112,128]{2,1,0:T(8,128)(2,1)}), bf16[64,112,128]{2,1,0:T(8,128)(2,1)S(1)}, u32[]{:S(2)}, u32[]{:S(2)}) async-start(bf16[64,112,128]{2,1,0:T(8,128)(2,1)} %shard_map.86), calls=%async_computation | async-start | bytes 3670016 | tf_op jit(solution)/shard_map/all_to_all | solution.py:269
  16.2 0.0 copy-done
  16.2 0.1 copy.9
  16.3 0.8 reshape.19.coef_ref
  17.2 19.8 %shard_map.89 = bf16[64,96,128]{2,1,0:T(8,128)(2,1)} custom-call(f32[2160]{0:T(1024)} %reshape.19.coef_ref, bf16[48,128,128]{2,1,0:T(8,128)(2,1)} %img_ref.1, bf16[48,128,128]{2,1,0:T(8,128)(2,1)} %var_ref.1, bf16[128,1152]{1,0:T(8,128)(2,1)} %constant.10.clone.xt_ref, bf16[128,1152]{1,0:T(8,128)(2,1)} %constant.11.clone.yt_ref), custom_call_target="tpu_custom_call" | custom-call | flops 6000000000 | bytes 6291456 | tf_op jit(solution)/shard_map/pallas_call | solution.py:270
  37.0 4.2 %all-to-all-done.got_ref = bf16[64,112,128]{2,1,0:T(8,128)(2,1)S(1)} async-done(((bf16[64,112,128]{2,1,0:T(8,128)(2,1)}), bf16[64,112,128]{2,1,0:T(8,128)(2,1)S(1)}, u32[]{:S(2)}, u32[]{:S(2)}) %all-to-all-start) | async-done | bytes 1835040 | tf_op jit(solution)/shard_map/all_to_all | solution.py:269
  41.2 5.8 %all-to-all-start.1 = ((bf16[64,96,128]{2,1,0:T(8,128)(2,1)}), bf16[64,96,128]{2,1,0:T(8,128)(2,1)S(1)}, u32[]{:S(2)}, u32[]{:S(2)}) async-start(bf16[64,96,128]{2,1,0:T(8,128)(2,1)} %shard_map.89), calls=%async_computation.1 | async-start | bytes 3145728 | tf_op jit(solution)/shard_map/all_to_all | solution.py:290
  46.9 2.9 %shard_map.87 = (s32[24,128]{1,0:T(8,128)S(1)}, bf16[256,256]{1,0:T(8,128)(2,1)S(1)}, bf16[256,256]{1,0:T(8,128)(2,1)}, bf16[256,256]{1,0:T(8,128)(2,1)}, bf16[256,256]{1,0:T(8,128)(2,1)}) custom-call(bf16[64,112,128]{2,1,0:T(8,128)(2,1)S(1)} %all-to-all-done.got_ref), custom_call_target="tpu_custom_call" | custom-call | tf_op jit(solution)/shard_map/pallas_call | solution.py:207
  49.8 6.0 %collective-permute-start = (bf16[256,256]{1,0:T(8,128)(2,1)}, bf16[256,256]{1,0:T(8,128)(2,1)S(1)}, u32[]{:S(2)}, u32[]{:S(2)}) collective-permute-start(bf16[256,256]{1,0:T(8,128)(2,1)} %get-tuple-element.12), channel_id=1, source_target_pairs={{0,32},{16,48},{32,0},{48,16},{1,33},{17,49},{33,1},{49,17},{2,34}... | collective-permute-start | bytes 393224 | tf_op jit(solution)/shard_map/ppermute | solution.py:218
  55.8 1.2 %collective-permute-start.1 = (bf16[256,256]{1,0:T(8,128)(2,1)}, bf16[256,256]{1,0:T(8,128)(2,1)S(1)}, u32[]{:S(2)}, u32[]{:S(2)}) collective-permute-start(bf16[256,256]{1,0:T(8,128)(2,1)} %get-tuple-element.13), channel_id=1, source_target_pairs={{0,16},{16,32},{32,48},{48,0},{1,17},{17,33},{33,49},{49,1},{2,18}... | collective-permute-start | bytes 393224 | tf_op jit(solution)/shard_map/ppermute | solution.py:218
  57.0 2.4 %collective-permute-start.2 = (bf16[256,256]{1,0:T(8,128)(2,1)}, bf16[256,256]{1,0:T(8,128)(2,1)S(1)}, u32[]{:S(2)}, u32[]{:S(2)}) collective-permute-start(bf16[256,256]{1,0:T(8,128)(2,1)} %get-tuple-element.14), channel_id=1, source_target_pairs={{0,48},{16,0},{32,16},{48,32},{1,49},{17,1},{33,17},{49,33},{2,50}... | collective-permute-start | bytes 393224 | tf_op jit(solution)/shard_map/ppermute | solution.py:218
  59.4 12.7 %all-to-all-done.1.got_ref = bf16[64,96,128]{2,1,0:T(8,128)(2,1)S(1)} async-done(((bf16[64,96,128]{2,1,0:T(8,128)(2,1)}), bf16[64,96,128]{2,1,0:T(8,128)(2,1)S(1)}, u32[]{:S(2)}, u32[]{:S(2)}) %all-to-all-start.1) | async-done | bytes 1572896 | tf_op jit(solution)/shard_map/all_to_all | solution.py:290
  72.1 2.0 %shard_map.90 = (bf16[256,256]{1,0:T(8,128)(2,1)S(1)}, bf16[256,256]{1,0:T(8,128)(2,1)S(1)}, bf16[256,256]{1,0:T(8,128)(2,1)S(1)}, bf16[256,256]{1,0:T(8,128)(2,1)S(1)}) custom-call(s32[24,128]{1,0:T(8,128)S(1)} %get-tuple-element.15.id_ref, bf16[64,96,128]{2,1,0:T(8,128)(2,1)S(1)} %all-to-all-done.1.got_ref), custom_call_target="tpu_custom_call" | custom-call | tf_op jit(solution)/shard_map/pallas_call | solution.py:199
  74.1 6.1 %collective-permute-start.3 = (bf16[256,256]{1,0:T(8,128)(2,1)S(1)}, bf16[256,256]{1,0:T(8,128)(2,1)S(1)}, u32[]{:S(2)}, u32[]{:S(2)}) collective-permute-start(bf16[256,256]{1,0:T(8,128)(2,1)S(1)} %get-tuple-element.17), channel_id=1, source_target_pairs={{0,32},{16,48},{32,0},{48,16},{1,33},{17,49},{33,1},{49,17},{2,34}... | collective-permute-start | bytes 393224 | tf_op jit(solution)/shard_map/ppermute | solution.py:218
  80.2 3.6 %collective-permute-start.4 = (bf16[256,256]{1,0:T(8,128)(2,1)S(1)}, bf16[256,256]{1,0:T(8,128)(2,1)S(1)}, u32[]{:S(2)}, u32[]{:S(2)}) collective-permute-start(bf16[256,256]{1,0:T(8,128)(2,1)S(1)} %get-tuple-element.18), channel_id=1, source_target_pairs={{0,16},{16,32},{32,48},{48,0},{1,17},{17,33},{33,49},{49,1},{2,18}... | collective-permute-start | bytes 393224 | tf_op jit(solution)/shard_map/ppermute | solution.py:218
  83.8 0.0 collective-permute-done.b_ref
  83.8 0.0 collective-permute-start.5
  83.8 0.0 collective-permute-done.1.c_ref
  83.8 0.0 collective-permute-done.2.d_ref
  83.8 0.1 shard_map.88.depth_ref
  83.9 0.0 collective-permute-done.3.b_ref
  83.9 9.4 %collective-permute-done.4.c_ref = bf16[256,256]{1,0:T(8,128)(2,1)S(1)} collective-permute-done((bf16[256,256]{1,0:T(8,128)(2,1)S(1)}, bf16[256,256]{1,0:T(8,128)(2,1)S(1)}, u32[]{:S(2)}, u32[]{:S(2)}) %collective-permute-start.4) | collective-permute-done | bytes 131104 | tf_op jit(solution)/shard_map/ppermute | solution.py:218
  93.3 0.7 collective-permute-done.5.d_ref
  93.9 0.3 shard_map.91
  94.2 16.5 %all_to_all.15.got_ref = bf16[64,16,128]{2,1,0:T(8,128)(2,1)S(1)} all-to-all(bf16[64,16,128]{2,1,0:T(8,128)(2,1)S(1)} %shard_map.91), channel_id=1, replica_groups=mesh['x'=4,'zh'=4,'zl'=2,'c'=2,'y'=4] {'x','zl','c','y'}, dimensions={0} | all-to-all | bytes 524288 | tf_op jit(solution)/shard_map/all_to_all | solution.py:308
  110.7 1.0 shard_map.92
Async XLA Ops:
  5.8 10.4 %copy-start = (f32[48,3,15]{0,2,1:T(8,128)S(1)}, f32[48,3,15]{0,2,1:T(8,128)}, u32[]{:S(2)}) copy-start(f32[48,3,15]{0,2,1:T(8,128)} %param.9) | copy-start | bytes 25924
  5.9 35.3 %all-to-all-start = ((bf16[64,112,128]{2,1,0:T(8,128)(2,1)}), bf16[64,112,128]{2,1,0:T(8,128)(2,1)S(1)}, u32[]{:S(2)}, u32[]{:S(2)}) async-start(bf16[64,112,128]{2,1,0:T(8,128)(2,1)} %shard_map.86), calls=%async_computation | async-start | bytes 3670016 | tf_op jit(solution)/shard_map/all_to_all | solution.py:269
  41.2 31.0 %all-to-all-start.1 = ((bf16[64,96,128]{2,1,0:T(8,128)(2,1)}), bf16[64,96,128]{2,1,0:T(8,128)(2,1)S(1)}, u32[]{:S(2)}, u32[]{:S(2)}) async-start(bf16[64,96,128]{2,1,0:T(8,128)(2,1)} %shard_map.89), calls=%async_computation.1 | async-start | bytes 3145728 | tf_op jit(solution)/shard_map/all_to_all | solution.py:290
  49.8 34.0 %collective-permute-start = (bf16[256,256]{1,0:T(8,128)(2,1)}, bf16[256,256]{1,0:T(8,128)(2,1)S(1)}, u32[]{:S(2)}, u32[]{:S(2)}) collective-permute-start(bf16[256,256]{1,0:T(8,128)(2,1)} %get-tuple-element.12), channel_id=1, source_target_pairs={{0,32},{16,48},{32,0},{48,16},{1,33},{17,49},{33,1},{49,17},{2,34}... | collective-permute-start | bytes 393224 | tf_op jit(solution)/shard_map/ppermute | solution.py:218
  55.8 28.0 %collective-permute-start.1 = (bf16[256,256]{1,0:T(8,128)(2,1)}, bf16[256,256]{1,0:T(8,128)(2,1)S(1)}, u32[]{:S(2)}, u32[]{:S(2)}) collective-permute-start(bf16[256,256]{1,0:T(8,128)(2,1)} %get-tuple-element.13), channel_id=1, source_target_pairs={{0,16},{16,32},{32,48},{48,0},{1,17},{17,33},{33,49},{49,1},{2,18}... | collective-permute-start | bytes 393224 | tf_op jit(solution)/shard_map/ppermute | solution.py:218
  57.0 26.9 %collective-permute-start.2 = (bf16[256,256]{1,0:T(8,128)(2,1)}, bf16[256,256]{1,0:T(8,128)(2,1)S(1)}, u32[]{:S(2)}, u32[]{:S(2)}) collective-permute-start(bf16[256,256]{1,0:T(8,128)(2,1)} %get-tuple-element.14), channel_id=1, source_target_pairs={{0,48},{16,0},{32,16},{48,32},{1,49},{17,1},{33,17},{49,33},{2,50}... | collective-permute-start | bytes 393224 | tf_op jit(solution)/shard_map/ppermute | solution.py:218
  74.1 9.8 %collective-permute-start.3 = (bf16[256,256]{1,0:T(8,128)(2,1)S(1)}, bf16[256,256]{1,0:T(8,128)(2,1)S(1)}, u32[]{:S(2)}, u32[]{:S(2)}) collective-permute-start(bf16[256,256]{1,0:T(8,128)(2,1)S(1)} %get-tuple-element.17), channel_id=1, source_target_pairs={{0,32},{16,48},{32,0},{48,16},{1,33},{17,49},{33,1},{49,17},{2,34}... | collective-permute-start | bytes 393224 | tf_op jit(solution)/shard_map/ppermute | solution.py:218
  80.2 13.1 %collective-permute-start.4 = (bf16[256,256]{1,0:T(8,128)(2,1)S(1)}, bf16[256,256]{1,0:T(8,128)(2,1)S(1)}, u32[]{:S(2)}, u32[]{:S(2)}) collective-permute-start(bf16[256,256]{1,0:T(8,128)(2,1)S(1)} %get-tuple-element.18), channel_id=1, source_target_pairs={{0,16},{16,32},{32,48},{48,0},{1,17},{17,33},{33,49},{49,1},{2,18}... | collective-permute-start | bytes 393224 | tf_op jit(solution)/shard_map/ppermute | solution.py:218
  83.8 10.1 %collective-permute-start.5 = (bf16[256,256]{1,0:T(8,128)(2,1)S(1)}, bf16[256,256]{1,0:T(8,128)(2,1)S(1)}, u32[]{:S(2)}, u32[]{:S(2)}) collective-permute-start(bf16[256,256]{1,0:T(8,128)(2,1)S(1)} %get-tuple-element.19), channel_id=1, source_target_pairs={{0,48},{16,0},{32,16},{48,32},{1,49},{17,1},{33,17},{49,33},{2,50}... | collective-permute-start | bytes 393224 | tf_op jit(solution)/shard_map/ppermute | solution.py:218

commit v4 on v3

--- a/solution.py
+++ b/solution.py
@@ -19,6 +19,7 @@
 ALL_BLOCKS = GROUP * HELD
 TILES = 256
 BATCH = 16
+STRIDE = 40
 STEP = 4
 LOADS = 8
 PARAMS = pltpu.CompilerParams(vmem_limit_bytes=56 * 2**20)
@@ -52,25 +53,22 @@
 
 def put(staged, i, value):
     for half in range(2):
-        staged[pl.ds(half * HELD + i, GROUP, stride=ROWS), :] = value[half * GROUP : (half + 1) * GROUP]
-
-
-def pack(staged, packed, out_hbm, sems):
-    def group(n):
-        copies = []
-        for half in range(2):
-            at = pl.ds(half * HELD + n * BATCH, BATCH)
-            for d in range(GROUP):
-                row = d * ROWS + half * HELD + n * BATCH
-                packed[d, at, :] = staged[row : row + BATCH, :].astype(jnp.bfloat16)
-            copies.append(pltpu.make_async_copy(packed.at[:, at, :], out_hbm.at[:, at, :], sems.at[2 * n + half]))
-            copies[-1].start()
-        return copies
-
-    return group
-
-
-def weigh_blocks(zh_ref, patch_hbm, slot_hbm, var_hbm, out_hbm, patch_ref, slot_ref, marks, var_ref, staged, packed, in_sems, sems):
+        staged[pl.ds(half * BATCH + i % BATCH, GROUP, stride=STRIDE), :] = value[half * GROUP : (half + 1) * GROUP]
+
+
+def pack(staged, packed, out_hbm, sems, n):
+    copies = []
+    for half in range(2):
+        at = pl.ds(n * BATCH + half * HELD, BATCH)
+        for d in range(GROUP):
+            row = d * STRIDE + half * BATCH
+            packed[d, at, :] = staged[row : row + BATCH, :].astype(jnp.bfloat16)
+        copies.append(pltpu.make_async_copy(packed.at[:, at, :], out_hbm.at[:, at, :], sems.at[2 * n + half]))
+        copies[-1].start()
+    return copies
+
+
+def weigh_blocks(zh_ref, patch_hbm, slot_hbm, var_hbm, out_hbm, patch_ref, slot_ref, marks, var_ref, packed, in_sems, sems, *staged):
     held = HELD // LOADS
     loads = []
     for n in range(LOADS):
@@ -96,13 +94,12 @@
     rows = pl.ds(ROWS, META)
     copies = [pltpu.make_async_copy(packed.at[:, rows, :], out_hbm.at[:, rows, :], sems.at[6])]
     copies[0].start()
-    group = pack(staged, packed, out_hbm, sems)
     for n in range(LOADS):
         loads[n].wait()
         for i in range(n * held, (n + 1) * held):
-            put(staged, i, pl.reciprocal(var_ref[i].astype(jnp.float32), approx=True))
+            put(staged[i // BATCH], i, pl.reciprocal(var_ref[i].astype(jnp.float32), approx=True))
             if i % BATCH == BATCH - 1:
-                copies += group(i // BATCH)
+                copies += pack(staged[i // BATCH], packed, out_hbm, sems, i // BATCH)
     for c in copies:
         c.wait()
 
@@ -141,13 +138,12 @@
         matched = both[:, :PIX] + v * both[:, PIX:]
         put(staged, step * STEP + n, matched / var_ref[n].astype(jnp.float32))
 
-    group = pack(staged, packed, out_hbm, sems)
     each = BATCH // STEP
     for n in range(HELD // BATCH):
 
         @pl.when(step == (n + 1) * each - 1)
         def _():
-            group(n)
+            pack(staged, packed, out_hbm, sems, n)
 
     @pl.when(step == last)
     def _():
@@ -245,7 +241,7 @@
 
 def local(images, variance, coefficients, patch_of, slot_of):
     x_table, y_table = tables()
-    scratch = [pltpu.VMEM((GROUP * ROWS, PIX), jnp.float32)]
+    scratch = [pltpu.VMEM((GROUP * STRIDE, PIX), jnp.float32)]
     weight_buf = pl.pallas_call(
         weigh_blocks,
         out_shape=jax.ShapeDtypeStruct((GROUP, ROWS + META, PIX), jnp.bfloat16),
@@ -256,13 +252,11 @@
             pltpu.VMEM((1, HELD), jnp.int32),
             pltpu.VMEM((META, PIX), jnp.float32),
             pltpu.VMEM((HELD, PIX, PIX), jnp.bfloat16),
-        ]
-        + scratch
-        + [
             pltpu.VMEM((GROUP, ROWS + META, PIX), jnp.bfloat16),
             pltpu.SemaphoreType.DMA((LOADS + 2,)),
             pltpu.SemaphoreType.DMA((7,)),
-        ],
+        ]
+        + scratch * (HELD // BATCH),
         compiler_params=PARAMS,
     )(lax.axis_index("zh").reshape(1), patch_of.reshape(1, HELD), slot_of.reshape(1, HELD), variance)
     group = ("x", "zl", "c", "y")

time: 112 us -> 110 us (0.982)
  Pallas kernels: 31.2 us -> 27 us
  waiting for transfers between devices: 26.9 us -> 28.8 us
    pallas_call x1, Pallas kernels: 5.2 us -> 2.85 us  [local(): pl.pallas_call(weigh_blocks, out_shape=jax.ShapeDtypeStruct((GROUP, ROWS...]
    all_to_all x1, waiting for transfers between devices: 4.18 us -> 6 us  [local(): lax.all_to_all(weight_buf, group, split_axis=0, concat_axis=0, tiled=True)]
    pallas_call x1, Pallas kernels: 19.8 us -> 18 us  [local(): pl.pallas_call(match_blocks, out_shape=jax.ShapeDtypeStruct((GROUP, ROWS,...]
  transfers between devices with their start and end apart: 8 -> 8, of which waited for: 4 -> 4; matrix products, arithmetic and copies ran while one was open for 1% -> 1% of each run, Pallas kernels for 22% -> 21%
where the time goes in v4:
time: 110 us; the launch traced here: 109 us
  starting transfers between devices  35.4 us (32%)
  waiting for transfers between devices  28.8 us (26%)
  Pallas kernels  27 us (25%)
  blocking collectives  16.5 us (15%)
    ppermute x6, starting transfers between devices, over_z(): return lax.ppermute(part, 'zh', [(i, (i + by) % 4) for i in range(4)])  19.3 us
    pallas_call x1, Pallas kernels, local(): pl.pallas_call(match_blocks, out_shape=jax.ShapeDtypeStruct((GROUP, ROWS,...  18 us
    all_to_all x1, blocking collectives, local(): lax.all_to_all(summed, group, split_axis=0, concat_axis=0, tiled=True)  16.5 us
    all_to_all x1, waiting for transfers between devices, local(): lax.all_to_all(matched_buf, group, split_axis=0, concat_axis=0, tiled=True)  12.7 us
    all_to_all x1, starting transfers between devices, local(): lax.all_to_all(weight_buf, group, split_axis=0, concat_axis=0, tiled=True)  10.4 us
    ppermute x6, waiting for transfers between devices, over_z(): return lax.ppermute(part, 'zh', [(i, (i + by) % 4) for i in range(4)])  10 us
    all_to_all x1, waiting for transfers between devices, local(): lax.all_to_all(weight_buf, group, split_axis=0, concat_axis=0, tiled=True)  6 us
    all_to_all x1, starting transfers between devices, local(): lax.all_to_all(matched_buf, group, split_axis=0, concat_axis=0, tiled=True)  5.75 us
  transfers between devices with their start and end apart: 8, of which 4 were waited for; matrix products, arithmetic and copies ran while one was open for 1% of the time, Pallas kernels for 21%

profile of v4, /device:TPU:1, one launch (start us, length us, event | category | flops | bytes accessed | tf_op | source)
XLA Modules:
  0.0 109.3 jit_solution(15567349266724789462)
XLA Ops:
  0.6 2.9 %shard_map.86 = bf16[64,112,128]{2,1,0:T(8,128)(2,1)} custom-call(s32[1]{0:T(128)} %bitcast.zh_ref, s32[1,48]{1,0:T(1,128)} %bitcast.3, s32[1,48]{1,0:T(1,128)} %bitcast.4, bf16[48,128,128]{2,1,0:T(8,128)(2,1)} %var_ref.1), custom_call_target="tpu_custom_call" | custom-call | tf_op jit(solution)/shard_map/pallas_call | solution.py:245
  3.5 0.0 copy-start
  3.5 10.4 %all-to-all-start = ((bf16[64,112,128]{2,1,0:T(8,128)(2,1)}), bf16[64,112,128]{2,1,0:T(8,128)(2,1)S(1)}, u32[]{:S(2)}, u32[]{:S(2)}) async-start(bf16[64,112,128]{2,1,0:T(8,128)(2,1)} %shard_map.86), calls=%async_computation | async-start | bytes 3670016 | tf_op jit(solution)/shard_map/all_to_all | solution.py:263
  13.9 0.0 copy-done
  13.9 0.1 copy.9
  14.0 0.8 reshape.19.coef_ref
  14.8 18.0 %shard_map.89 = bf16[64,96,128]{2,1,0:T(8,128)(2,1)} custom-call(f32[2160]{0:T(1024)} %reshape.19.coef_ref, bf16[48,128,128]{2,1,0:T(8,128)(2,1)} %img_ref.1, bf16[48,128,128]{2,1,0:T(8,128)(2,1)} %var_ref.1, bf16[128,1152]{1,0:T(8,128)(2,1)} %constant.10.clone.xt_ref, bf16[128,1152]{1,0:T(8,128)(2,1)} %constant.11.clone.yt_ref), custom_call_target="tpu_custom_call" | custom-call | flops 6000000000 | bytes 6291456 | tf_op jit(solution)/shard_map/pallas_call | solution.py:264
  32.8 6.0 %all-to-all-done.got_ref = bf16[64,112,128]{2,1,0:T(8,128)(2,1)S(1)} async-done(((bf16[64,112,128]{2,1,0:T(8,128)(2,1)}), bf16[64,112,128]{2,1,0:T(8,128)(2,1)S(1)}, u32[]{:S(2)}, u32[]{:S(2)}) %all-to-all-start) | async-done | bytes 1835040 | tf_op jit(solution)/shard_map/all_to_all | solution.py:263
  38.8 5.8 %all-to-all-start.1 = ((bf16[64,96,128]{2,1,0:T(8,128)(2,1)}), bf16[64,96,128]{2,1,0:T(8,128)(2,1)S(1)}, u32[]{:S(2)}, u32[]{:S(2)}) async-start(bf16[64,96,128]{2,1,0:T(8,128)(2,1)} %shard_map.89), calls=%async_computation.1 | async-start | bytes 3145728 | tf_op jit(solution)/shard_map/all_to_all | solution.py:284
  44.6 2.9 %shard_map.87 = (s32[24,128]{1,0:T(8,128)S(1)}, bf16[256,256]{1,0:T(8,128)(2,1)S(1)}, bf16[256,256]{1,0:T(8,128)(2,1)}, bf16[256,256]{1,0:T(8,128)(2,1)}, bf16[256,256]{1,0:T(8,128)(2,1)}) custom-call(bf16[64,112,128]{2,1,0:T(8,128)(2,1)S(1)} %all-to-all-done.got_ref), custom_call_target="tpu_custom_call" | custom-call | tf_op jit(solution)/shard_map/pallas_call | solution.py:203
  47.4 6.0 %collective-permute-start = (bf16[256,256]{1,0:T(8,128)(2,1)}, bf16[256,256]{1,0:T(8,128)(2,1)S(1)}, u32[]{:S(2)}, u32[]{:S(2)}) collective-permute-start(bf16[256,256]{1,0:T(8,128)(2,1)} %get-tuple-element.12), channel_id=1, source_target_pairs={{0,32},{16,48},{32,0},{48,16},{1,33},{17,49},{33,1},{49,17},{2,34}... | collective-permute-start | bytes 393224 | tf_op jit(solution)/shard_map/ppermute | solution.py:214
  53.4 1.2 %collective-permute-start.1 = (bf16[256,256]{1,0:T(8,128)(2,1)}, bf16[256,256]{1,0:T(8,128)(2,1)S(1)}, u32[]{:S(2)}, u32[]{:S(2)}) collective-permute-start(bf16[256,256]{1,0:T(8,128)(2,1)} %get-tuple-element.13), channel_id=1, source_target_pairs={{0,16},{16,32},{32,48},{48,0},{1,17},{17,33},{33,49},{49,1},{2,18}... | collective-permute-start | bytes 393224 | tf_op jit(solution)/shard_map/ppermute | solution.py:214
  54.6 2.4 %collective-permute-start.2 = (bf16[256,256]{1,0:T(8,128)(2,1)}, bf16[256,256]{1,0:T(8,128)(2,1)S(1)}, u32[]{:S(2)}, u32[]{:S(2)}) collective-permute-start(bf16[256,256]{1,0:T(8,128)(2,1)} %get-tuple-element.14), channel_id=1, source_target_pairs={{0,48},{16,0},{32,16},{48,32},{1,49},{17,1},{33,17},{49,33},{2,50}... | collective-permute-start | bytes 393224 | tf_op jit(solution)/shard_map/ppermute | solution.py:214
  57.0 12.7 %all-to-all-done.1.got_ref = bf16[64,96,128]{2,1,0:T(8,128)(2,1)S(1)} async-done(((bf16[64,96,128]{2,1,0:T(8,128)(2,1)}), bf16[64,96,128]{2,1,0:T(8,128)(2,1)S(1)}, u32[]{:S(2)}, u32[]{:S(2)}) %all-to-all-start.1) | async-done | bytes 1572896 | tf_op jit(solution)/shard_map/all_to_all | solution.py:284
  69.8 2.0 %shard_map.90 = (bf16[256,256]{1,0:T(8,128)(2,1)S(1)}, bf16[256,256]{1,0:T(8,128)(2,1)S(1)}, bf16[256,256]{1,0:T(8,128)(2,1)S(1)}, bf16[256,256]{1,0:T(8,128)(2,1)S(1)}) custom-call(s32[24,128]{1,0:T(8,128)S(1)} %get-tuple-element.15.id_ref, bf16[64,96,128]{2,1,0:T(8,128)(2,1)S(1)} %all-to-all-done.1.got_ref), custom_call_target="tpu_custom_call" | custom-call | tf_op jit(solution)/shard_map/pallas_call | solution.py:195
  71.8 6.1 %collective-permute-start.3 = (bf16[256,256]{1,0:T(8,128)(2,1)S(1)}, bf16[256,256]{1,0:T(8,128)(2,1)S(1)}, u32[]{:S(2)}, u32[]{:S(2)}) collective-permute-start(bf16[256,256]{1,0:T(8,128)(2,1)S(1)} %get-tuple-element.17), channel_id=1, source_target_pairs={{0,32},{16,48},{32,0},{48,16},{1,33},{17,49},{33,1},{49,17},{2,34}... | collective-permute-start | bytes 393224 | tf_op jit(solution)/shard_map/ppermute | solution.py:214
  77.9 3.6 %collective-permute-start.4 = (bf16[256,256]{1,0:T(8,128)(2,1)S(1)}, bf16[256,256]{1,0:T(8,128)(2,1)S(1)}, u32[]{:S(2)}, u32[]{:S(2)}) collective-permute-start(bf16[256,256]{1,0:T(8,128)(2,1)S(1)} %get-tuple-element.18), channel_id=1, source_target_pairs={{0,16},{16,32},{32,48},{48,0},{1,17},{17,33},{33,49},{49,1},{2,18}... | collective-permute-start | bytes 393224 | tf_op jit(solution)/shard_map/ppermute | solution.py:214
  81.5 0.0 collective-permute-done.b_ref
  81.5 0.0 collective-permute-start.5
  81.5 0.0 collective-permute-done.1.c_ref
  81.5 0.0 collective-permute-done.2.d_ref
  81.5 0.1 shard_map.88.depth_ref
  81.6 0.0 collective-permute-done.3.b_ref
  81.6 9.4 %collective-permute-done.4.c_ref = bf16[256,256]{1,0:T(8,128)(2,1)S(1)} collective-permute-done((bf16[256,256]{1,0:T(8,128)(2,1)S(1)}, bf16[256,256]{1,0:T(8,128)(2,1)S(1)}, u32[]{:S(2)}, u32[]{:S(2)}) %collective-permute-start.4) | collective-permute-done | bytes 131104 | tf_op jit(solution)/shard_map/ppermute | solution.py:214
  90.9 0.7 collective-permute-done.5.d_ref
  91.6 0.3 shard_map.91
  91.9 16.5 %all_to_all.15.got_ref = bf16[64,16,128]{2,1,0:T(8,128)(2,1)S(1)} all-to-all(bf16[64,16,128]{2,1,0:T(8,128)(2,1)S(1)} %shard_map.91), channel_id=1, replica_groups=mesh['x'=4,'zh'=4,'zl'=2,'c'=2,'y'=4] {'x','zl','c','y'}, dimensions={0} | all-to-all | bytes 524288 | tf_op jit(solution)/shard_map/all_to_all | solution.py:302
  108.3 1.0 shard_map.92
Async XLA Ops:
  3.5 10.4 %copy-start = (f32[48,3,15]{0,2,1:T(8,128)S(1)}, f32[48,3,15]{0,2,1:T(8,128)}, u32[]{:S(2)}) copy-start(f32[48,3,15]{0,2,1:T(8,128)} %param.9) | copy-start | bytes 25924
  3.5 35.3 %all-to-all-start = ((bf16[64,112,128]{2,1,0:T(8,128)(2,1)}), bf16[64,112,128]{2,1,0:T(8,128)(2,1)S(1)}, u32[]{:S(2)}, u32[]{:S(2)}) async-start(bf16[64,112,128]{2,1,0:T(8,128)(2,1)} %shard_map.86), calls=%async_computation | async-start | bytes 3670016 | tf_op jit(solution)/shard_map/all_to_all | solution.py:263
  38.8 31.0 %all-to-all-start.1 = ((bf16[64,96,128]{2,1,0:T(8,128)(2,1)}), bf16[64,96,128]{2,1,0:T(8,128)(2,1)S(1)}, u32[]{:S(2)}, u32[]{:S(2)}) async-start(bf16[64,96,128]{2,1,0:T(8,128)(2,1)} %shard_map.89), calls=%async_computation.1 | async-start | bytes 3145728 | tf_op jit(solution)/shard_map/all_to_all | solution.py:284
  47.4 34.0 %collective-permute-start = (bf16[256,256]{1,0:T(8,128)(2,1)}, bf16[256,256]{1,0:T(8,128)(2,1)S(1)}, u32[]{:S(2)}, u32[]{:S(2)}) collective-permute-start(bf16[256,256]{1,0:T(8,128)(2,1)} %get-tuple-element.12), channel_id=1, source_target_pairs={{0,32},{16,48},{32,0},{48,16},{1,33},{17,49},{33,1},{49,17},{2,34}... | collective-permute-start | bytes 393224 | tf_op jit(solution)/shard_map/ppermute | solution.py:214
  53.4 28.0 %collective-permute-start.1 = (bf16[256,256]{1,0:T(8,128)(2,1)}, bf16[256,256]{1,0:T(8,128)(2,1)S(1)}, u32[]{:S(2)}, u32[]{:S(2)}) collective-permute-start(bf16[256,256]{1,0:T(8,128)(2,1)} %get-tuple-element.13), channel_id=1, source_target_pairs={{0,16},{16,32},{32,48},{48,0},{1,17},{17,33},{33,49},{49,1},{2,18}... | collective-permute-start | bytes 393224 | tf_op jit(solution)/shard_map/ppermute | solution.py:214
  54.6 26.8 %collective-permute-start.2 = (bf16[256,256]{1,0:T(8,128)(2,1)}, bf16[256,256]{1,0:T(8,128)(2,1)S(1)}, u32[]{:S(2)}, u32[]{:S(2)}) collective-permute-start(bf16[256,256]{1,0:T(8,128)(2,1)} %get-tuple-element.14), channel_id=1, source_target_pairs={{0,48},{16,0},{32,16},{48,32},{1,49},{17,1},{33,17},{49,33},{2,50}... | collective-permute-start | bytes 393224 | tf_op jit(solution)/shard_map/ppermute | solution.py:214
  71.8 9.8 %collective-permute-start.3 = (bf16[256,256]{1,0:T(8,128)(2,1)S(1)}, bf16[256,256]{1,0:T(8,128)(2,1)S(1)}, u32[]{:S(2)}, u32[]{:S(2)}) collective-permute-start(bf16[256,256]{1,0:T(8,128)(2,1)S(1)} %get-tuple-element.17), channel_id=1, source_target_pairs={{0,32},{16,48},{32,0},{48,16},{1,33},{17,49},{33,1},{49,17},{2,34}... | collective-permute-start | bytes 393224 | tf_op jit(solution)/shard_map/ppermute | solution.py:214
  77.9 13.1 %collective-permute-start.4 = (bf16[256,256]{1,0:T(8,128)(2,1)S(1)}, bf16[256,256]{1,0:T(8,128)(2,1)S(1)}, u32[]{:S(2)}, u32[]{:S(2)}) collective-permute-start(bf16[256,256]{1,0:T(8,128)(2,1)S(1)} %get-tuple-element.18), channel_id=1, source_target_pairs={{0,16},{16,32},{32,48},{48,0},{1,17},{17,33},{33,49},{49,1},{2,18}... | collective-permute-start | bytes 393224 | tf_op jit(solution)/shard_map/ppermute | solution.py:214
  81.5 10.1 %collective-permute-start.5 = (bf16[256,256]{1,0:T(8,128)(2,1)S(1)}, bf16[256,256]{1,0:T(8,128)(2,1)S(1)}, u32[]{:S(2)}, u32[]{:S(2)}) collective-permute-start(bf16[256,256]{1,0:T(8,128)(2,1)S(1)} %get-tuple-element.19), channel_id=1, source_target_pairs={{0,48},{16,0},{32,16},{48,32},{1,49},{17,1},{33,17},{49,33},{2,50}... | collective-permute-start | bytes 393224 | tf_op jit(solution)/shard_map/ppermute | solution.py:214

commit v5 on v4

--- a/solution.py
+++ b/solution.py
@@ -19,6 +19,7 @@
 ALL_BLOCKS = GROUP * HELD
 TILES = 256
 BATCH = 16
+TURN = 24
 STRIDE = 40
 STEP = 4
 LOADS = 8
@@ -83,7 +84,7 @@
     patch, slot = patch_ref[...], slot_ref[...]
     z_at = (patch // 2) % 8
     z_by = (z_at // 2 + 4 - zh_ref[0]) % 4
-    owner = ((patch // 16 * 2 + z_at % 2) * 2 + patch % 2) * 4 + slot // 4
+    owner = ((z_at % 2 * 2 + patch % 2) * 4 + patch // 16) * 4 + slot // 4
     tile = (z_by * 4 + slot % 4) * GROUP + owner
     low = lax.broadcasted_iota(jnp.int32, (META, HELD), 0) < META // 2
     marks[...] = jnp.zeros_like(marks)
@@ -223,18 +224,20 @@
     for n, total in enumerate((depth_ref[...], num)):
         for half in range(2):
             for s in range(4):
-                at = pl.ds((2 * n + half) * 4 + s, GROUP, stride=16)
+                at = pl.ds((2 * n + half) * 4 + s, GROUP, stride=TURN)
                 turned[at, :] = total[s * GROUP : (s + 1) * GROUP, half * PIX : (half + 1) * PIX]
-    out_ref[...] = turned[...].astype(jnp.bfloat16).reshape(GROUP, 16, PIX)
+    for d in range(GROUP):
+        out_ref[d] = turned[d * TURN : d * TURN + 16, :].astype(jnp.bfloat16)
 
 
 def combine(got_ref, coadd_ref, depth_ref, flat):
-    flat[...] = got_ref[...].astype(jnp.float32).reshape(GROUP * 16, PIX)
+    for d in range(GROUP):
+        flat[d * TURN : d * TURN + 16, :] = got_ref[d].astype(jnp.float32)
     for s in range(4):
         for half in range(2):
             rows = slice(half * GROUP, (half + 1) * GROUP)
-            depth = flat[pl.ds(half * 4 + s, GROUP, stride=16), :]
-            num = flat[pl.ds((2 + half) * 4 + s, GROUP, stride=16), :]
+            depth = flat[pl.ds(half * 4 + s, GROUP, stride=TURN), :]
+            num = flat[pl.ds((2 + half) * 4 + s, GROUP, stride=TURN), :]
             depth_ref[s, rows, :] = depth
             coadd_ref[s, rows, :] = num / jnp.maximum(depth, 1.0)
 
@@ -259,7 +262,7 @@
         + scratch * (HELD // BATCH),
         compiler_params=PARAMS,
     )(lax.axis_index("zh").reshape(1), patch_of.reshape(1, HELD), slot_of.reshape(1, HELD), variance)
-    group = ("x", "zl", "c", "y")
+    group = ("zl", "c", "x", "y")
     weight_got = lax.all_to_all(weight_buf, group, split_axis=0, concat_axis=0, tiled=True)
     matched_buf = pl.pallas_call(
         match_blocks,
@@ -296,7 +299,7 @@
         out_shape=jax.ShapeDtypeStruct((GROUP, 16, PIX), jnp.bfloat16),
         in_specs=[VMEM_SPEC] * 5,
         out_specs=VMEM_SPEC,
-        scratch_shapes=[pltpu.VMEM((GROUP * 16, PIX), jnp.float32)],
+        scratch_shapes=[pltpu.VMEM((GROUP * TURN, PIX), jnp.float32)],
         compiler_params=ADD_PARAMS,
     )(depth, own, over_z(far, 2), over_z(up, 1), over_z(down, 3))
     whole = lax.all_to_all(summed, group, split_axis=0, concat_axis=0, tiled=True)
@@ -306,7 +309,7 @@
         out_shape=(out, out),
         in_specs=[VMEM_SPEC],
         out_specs=(VMEM_SPEC, VMEM_SPEC),
-        scratch_shapes=[pltpu.VMEM((GROUP * 16, PIX), jnp.float32)],
+        scratch_shapes=[pltpu.VMEM((GROUP * TURN, PIX), jnp.float32)],
         compiler_params=ADD_PARAMS,
     )(whole)
 

time: 110 us -> 109 us (level)
  waiting for transfers between devices: 28.8 us -> 27.5 us
where the time goes in v5:
time: 109 us
  starting transfers between devices  35.8 us (33%)
  waiting for transfers between devices  27.5 us (25%)
  Pallas kernels  26.8 us (25%)
  blocking collectives  17.1 us (16%)
    ppermute x6, starting transfers between devices, over_z(): return lax.ppermute(part, 'zh', [(i, (i + by) % 4) for i in range(4)])  19.5 us
    pallas_call x1, Pallas kernels, local(): pl.pallas_call(match_blocks, out_shape=jax.ShapeDtypeStruct((GROUP, ROWS,...  18 us
    all_to_all x1, blocking collectives, local(): lax.all_to_all(summed, group, split_axis=0, concat_axis=0, tiled=True)  17.1 us
    all_to_all x1, waiting for transfers between devices, local(): lax.all_to_all(matched_buf, group, split_axis=0, concat_axis=0, tiled=True)  12 us
    all_to_all x1, starting transfers between devices, local(): lax.all_to_all(weight_buf, group, split_axis=0, concat_axis=0, tiled=True)  10.4 us
    ppermute x6, waiting for transfers between devices, over_z(): return lax.ppermute(part, 'zh', [(i, (i + by) % 4) for i in range(4)])  9.78 us
    all_to_all x1, starting transfers between devices, local(): lax.all_to_all(matched_buf, group, split_axis=0, concat_axis=0, tiled=True)  5.9 us
    all_to_all x1, waiting for transfers between devices, local(): lax.all_to_all(weight_buf, group, split_axis=0, concat_axis=0, tiled=True)  5.72 us
  transfers between devices with their start and end apart: 8, of which 4 were waited for; matrix products, arithmetic and copies ran while one was open for 1% of the time, Pallas kernels for 21%

profile of v5, /device:TPU:1, one launch (start us, length us, event | category | flops | bytes accessed | tf_op | source)
XLA Modules:
  0.0 108.9 jit_solution(3764187109330763488)
XLA Ops:
  0.6 2.9 %shard_map.86 = bf16[64,112,128]{2,1,0:T(8,128)(2,1)} custom-call(s32[1]{0:T(128)} %bitcast.zh_ref, s32[1,48]{1,0:T(1,128)} %bitcast.3, s32[1,48]{1,0:T(1,128)} %bitcast.4, bf16[48,128,128]{2,1,0:T(8,128)(2,1)} %var_ref.1), custom_call_target="tpu_custom_call" | custom-call | tf_op jit(solution)/shard_map/pallas_call | solution.py:248
  3.5 0.0 copy-start
  3.5 10.4 %all-to-all-start = ((bf16[64,112,128]{2,1,0:T(8,128)(2,1)}), bf16[64,112,128]{2,1,0:T(8,128)(2,1)S(1)}, u32[]{:S(2)}, u32[]{:S(2)}) async-start(bf16[64,112,128]{2,1,0:T(8,128)(2,1)} %shard_map.86), calls=%async_computation | async-start | bytes 3670016 | tf_op jit(solution)/shard_map/all_to_all | solution.py:266
  13.9 0.0 copy-done
  13.9 0.1 copy.9
  14.0 0.8 reshape.19.coef_ref
  14.8 18.0 %shard_map.89 = bf16[64,96,128]{2,1,0:T(8,128)(2,1)} custom-call(f32[2160]{0:T(1024)} %reshape.19.coef_ref, bf16[48,128,128]{2,1,0:T(8,128)(2,1)} %img_ref.1, bf16[48,128,128]{2,1,0:T(8,128)(2,1)} %var_ref.1, bf16[128,1152]{1,0:T(8,128)(2,1)} %constant.10.clone.xt_ref, bf16[128,1152]{1,0:T(8,128)(2,1)} %constant.11.clone.yt_ref), custom_call_target="tpu_custom_call" | custom-call | flops 6000000000 | bytes 6291456 | tf_op jit(solution)/shard_map/pallas_call | solution.py:267
  32.8 5.7 %all-to-all-done.got_ref = bf16[64,112,128]{2,1,0:T(8,128)(2,1)S(1)} async-done(((bf16[64,112,128]{2,1,0:T(8,128)(2,1)}), bf16[64,112,128]{2,1,0:T(8,128)(2,1)S(1)}, u32[]{:S(2)}, u32[]{:S(2)}) %all-to-all-start) | async-done | bytes 1835040 | tf_op jit(solution)/shard_map/all_to_all | solution.py:266
  38.5 5.9 %all-to-all-start.1 = ((bf16[64,96,128]{2,1,0:T(8,128)(2,1)}), bf16[64,96,128]{2,1,0:T(8,128)(2,1)S(1)}, u32[]{:S(2)}, u32[]{:S(2)}) async-start(bf16[64,96,128]{2,1,0:T(8,128)(2,1)} %shard_map.89), calls=%async_computation.1 | async-start | bytes 3145728 | tf_op jit(solution)/shard_map/all_to_all | solution.py:287
  44.4 2.9 %shard_map.87 = (s32[24,128]{1,0:T(8,128)S(1)}, bf16[256,256]{1,0:T(8,128)(2,1)S(1)}, bf16[256,256]{1,0:T(8,128)(2,1)}, bf16[256,256]{1,0:T(8,128)(2,1)}, bf16[256,256]{1,0:T(8,128)(2,1)}) custom-call(bf16[64,112,128]{2,1,0:T(8,128)(2,1)S(1)} %all-to-all-done.got_ref), custom_call_target="tpu_custom_call" | custom-call | tf_op jit(solution)/shard_map/pallas_call | solution.py:204
  47.3 6.0 %collective-permute-start = (bf16[256,256]{1,0:T(8,128)(2,1)}, bf16[256,256]{1,0:T(8,128)(2,1)S(1)}, u32[]{:S(2)}, u32[]{:S(2)}) collective-permute-start(bf16[256,256]{1,0:T(8,128)(2,1)} %get-tuple-element.12), channel_id=1, source_target_pairs={{0,32},{16,48},{32,0},{48,16},{1,33},{17,49},{33,1},{49,17},{2,34}... | collective-permute-start | bytes 393224 | tf_op jit(solution)/shard_map/ppermute | solution.py:215
  53.3 1.2 %collective-permute-start.1 = (bf16[256,256]{1,0:T(8,128)(2,1)}, bf16[256,256]{1,0:T(8,128)(2,1)S(1)}, u32[]{:S(2)}, u32[]{:S(2)}) collective-permute-start(bf16[256,256]{1,0:T(8,128)(2,1)} %get-tuple-element.13), channel_id=1, source_target_pairs={{0,16},{16,32},{32,48},{48,0},{1,17},{17,33},{33,49},{49,1},{2,18}... | collective-permute-start | bytes 393224 | tf_op jit(solution)/shard_map/ppermute | solution.py:215
  54.5 2.4 %collective-permute-start.2 = (bf16[256,256]{1,0:T(8,128)(2,1)}, bf16[256,256]{1,0:T(8,128)(2,1)S(1)}, u32[]{:S(2)}, u32[]{:S(2)}) collective-permute-start(bf16[256,256]{1,0:T(8,128)(2,1)} %get-tuple-element.14), channel_id=1, source_target_pairs={{0,48},{16,0},{32,16},{48,32},{1,49},{17,1},{33,17},{49,33},{2,50}... | collective-permute-start | bytes 393224 | tf_op jit(solution)/shard_map/ppermute | solution.py:215
  56.9 12.0 %all-to-all-done.1.got_ref = bf16[64,96,128]{2,1,0:T(8,128)(2,1)S(1)} async-done(((bf16[64,96,128]{2,1,0:T(8,128)(2,1)}), bf16[64,96,128]{2,1,0:T(8,128)(2,1)S(1)}, u32[]{:S(2)}, u32[]{:S(2)}) %all-to-all-start.1) | async-done | bytes 1572896 | tf_op jit(solution)/shard_map/all_to_all | solution.py:287
  68.9 2.0 %shard_map.90 = (bf16[256,256]{1,0:T(8,128)(2,1)S(1)}, bf16[256,256]{1,0:T(8,128)(2,1)S(1)}, bf16[256,256]{1,0:T(8,128)(2,1)S(1)}, bf16[256,256]{1,0:T(8,128)(2,1)S(1)}) custom-call(s32[24,128]{1,0:T(8,128)S(1)} %get-tuple-element.15.id_ref, bf16[64,96,128]{2,1,0:T(8,128)(2,1)S(1)} %all-to-all-done.1.got_ref), custom_call_target="tpu_custom_call" | custom-call | tf_op jit(solution)/shard_map/pallas_call | solution.py:196
  70.9 6.1 %collective-permute-start.3 = (bf16[256,256]{1,0:T(8,128)(2,1)S(1)}, bf16[256,256]{1,0:T(8,128)(2,1)S(1)}, u32[]{:S(2)}, u32[]{:S(2)}) collective-permute-start(bf16[256,256]{1,0:T(8,128)(2,1)S(1)} %get-tuple-element.17), channel_id=1, source_target_pairs={{0,32},{16,48},{32,0},{48,16},{1,33},{17,49},{33,1},{49,17},{2,34}... | collective-permute-start | bytes 393224 | tf_op jit(solution)/shard_map/ppermute | solution.py:215
  77.0 3.8 %collective-permute-start.4 = (bf16[256,256]{1,0:T(8,128)(2,1)S(1)}, bf16[256,256]{1,0:T(8,128)(2,1)S(1)}, u32[]{:S(2)}, u32[]{:S(2)}) collective-permute-start(bf16[256,256]{1,0:T(8,128)(2,1)S(1)} %get-tuple-element.18), channel_id=1, source_target_pairs={{0,16},{16,32},{32,48},{48,0},{1,17},{17,33},{33,49},{49,1},{2,18}... | collective-permute-start | bytes 393224 | tf_op jit(solution)/shard_map/ppermute | solution.py:215
  80.8 0.0 collective-permute-done.b_ref
  80.8 0.0 collective-permute-start.5
  80.8 0.0 collective-permute-done.1.c_ref
  80.8 0.0 collective-permute-done.2.d_ref
  80.9 0.1 shard_map.88.depth_ref
  80.9 2.4 %collective-permute-done.3.b_ref = bf16[256,256]{1,0:T(8,128)(2,1)S(1)} collective-permute-done((bf16[256,256]{1,0:T(8,128)(2,1)S(1)}, bf16[256,256]{1,0:T(8,128)(2,1)S(1)}, u32[]{:S(2)}, u32[]{:S(2)}) %collective-permute-start.3) | collective-permute-done | bytes 131104 | tf_op jit(solution)/shard_map/ppermute | solution.py:215
  83.3 7.4 %collective-permute-done.4.c_ref = bf16[256,256]{1,0:T(8,128)(2,1)S(1)} collective-permute-done((bf16[256,256]{1,0:T(8,128)(2,1)S(1)}, bf16[256,256]{1,0:T(8,128)(2,1)S(1)}, u32[]{:S(2)}, u32[]{:S(2)}) %collective-permute-start.4) | collective-permute-done | bytes 131104 | tf_op jit(solution)/shard_map/ppermute | solution.py:215
  90.7 0.0 collective-permute-done.5.d_ref
  90.7 0.2 shard_map.91
  90.9 17.1 %all_to_all.15.got_ref = bf16[64,16,128]{2,1,0:T(8,128)(2,1)S(1)} all-to-all(bf16[64,16,128]{2,1,0:T(8,128)(2,1)S(1)} %shard_map.91), channel_id=1, replica_groups=mesh['x'=4,'zh'=4,'zl'=2,'c'=2,'y'=4] {'zl','c','x','y'}, dimensions={0} | all-to-all | bytes 524288 | tf_op jit(solution)/shard_map/all_to_all | solution.py:305
  108.0 0.9 shard_map.92
Async XLA Ops:
  3.5 10.4 %copy-start = (f32[48,3,15]{0,2,1:T(8,128)S(1)}, f32[48,3,15]{0,2,1:T(8,128)}, u32[]{:S(2)}) copy-start(f32[48,3,15]{0,2,1:T(8,128)} %param.9) | copy-start | bytes 25924
  3.5 35.0 %all-to-all-start = ((bf16[64,112,128]{2,1,0:T(8,128)(2,1)}), bf16[64,112,128]{2,1,0:T(8,128)(2,1)S(1)}, u32[]{:S(2)}, u32[]{:S(2)}) async-start(bf16[64,112,128]{2,1,0:T(8,128)(2,1)} %shard_map.86), calls=%async_computation | async-start | bytes 3670016 | tf_op jit(solution)/shard_map/all_to_all | solution.py:266
  38.5 30.4 %all-to-all-start.1 = ((bf16[64,96,128]{2,1,0:T(8,128)(2,1)}), bf16[64,96,128]{2,1,0:T(8,128)(2,1)S(1)}, u32[]{:S(2)}, u32[]{:S(2)}) async-start(bf16[64,96,128]{2,1,0:T(8,128)(2,1)} %shard_map.89), calls=%async_computation.1 | async-start | bytes 3145728 | tf_op jit(solution)/shard_map/all_to_all | solution.py:287
  47.3 33.5 %collective-permute-start = (bf16[256,256]{1,0:T(8,128)(2,1)}, bf16[256,256]{1,0:T(8,128)(2,1)S(1)}, u32[]{:S(2)}, u32[]{:S(2)}) collective-permute-start(bf16[256,256]{1,0:T(8,128)(2,1)} %get-tuple-element.12), channel_id=1, source_target_pairs={{0,32},{16,48},{32,0},{48,16},{1,33},{17,49},{33,1},{49,17},{2,34}... | collective-permute-start | bytes 393224 | tf_op jit(solution)/shard_map/ppermute | solution.py:215
  53.3 27.5 %collective-permute-start.1 = (bf16[256,256]{1,0:T(8,128)(2,1)}, bf16[256,256]{1,0:T(8,128)(2,1)S(1)}, u32[]{:S(2)}, u32[]{:S(2)}) collective-permute-start(bf16[256,256]{1,0:T(8,128)(2,1)} %get-tuple-element.13), channel_id=1, source_target_pairs={{0,16},{16,32},{32,48},{48,0},{1,17},{17,33},{33,49},{49,1},{2,18}... | collective-permute-start | bytes 393224 | tf_op jit(solution)/shard_map/ppermute | solution.py:215
  54.5 26.3 %collective-permute-start.2 = (bf16[256,256]{1,0:T(8,128)(2,1)}, bf16[256,256]{1,0:T(8,128)(2,1)S(1)}, u32[]{:S(2)}, u32[]{:S(2)}) collective-permute-start(bf16[256,256]{1,0:T(8,128)(2,1)} %get-tuple-element.14), channel_id=1, source_target_pairs={{0,48},{16,0},{32,16},{48,32},{1,49},{17,1},{33,17},{49,33},{2,50}... | collective-permute-start | bytes 393224 | tf_op jit(solution)/shard_map/ppermute | solution.py:215
  70.9 12.4 %collective-permute-start.3 = (bf16[256,256]{1,0:T(8,128)(2,1)S(1)}, bf16[256,256]{1,0:T(8,128)(2,1)S(1)}, u32[]{:S(2)}, u32[]{:S(2)}) collective-permute-start(bf16[256,256]{1,0:T(8,128)(2,1)S(1)} %get-tuple-element.17), channel_id=1, source_target_pairs={{0,32},{16,48},{32,0},{48,16},{1,33},{17,49},{33,1},{49,17},{2,34}... | collective-permute-start | bytes 393224 | tf_op jit(solution)/shard_map/ppermute | solution.py:215
  77.0 13.7 %collective-permute-start.4 = (bf16[256,256]{1,0:T(8,128)(2,1)S(1)}, bf16[256,256]{1,0:T(8,128)(2,1)S(1)}, u32[]{:S(2)}, u32[]{:S(2)}) collective-permute-start(bf16[256,256]{1,0:T(8,128)(2,1)S(1)} %get-tuple-element.18), channel_id=1, source_target_pairs={{0,16},{16,32},{32,48},{48,0},{1,17},{17,33},{33,49},{49,1},{2,18}... | collective-permute-start | bytes 393224 | tf_op jit(solution)/shard_map/ppermute | solution.py:215
  80.8 9.9 %collective-permute-start.5 = (bf16[256,256]{1,0:T(8,128)(2,1)S(1)}, bf16[256,256]{1,0:T(8,128)(2,1)S(1)}, u32[]{:S(2)}, u32[]{:S(2)}) collective-permute-start(bf16[256,256]{1,0:T(8,128)(2,1)S(1)} %get-tuple-element.19), channel_id=1, source_target_pairs={{0,48},{16,0},{32,16},{48,32},{1,49},{17,1},{33,17},{49,33},{2,50}... | collective-permute-start | bytes 393224 | tf_op jit(solution)/shard_map/ppermute | solution.py:215

commit v6 on v5

--- a/solution.py
+++ b/solution.py
@@ -173,7 +173,7 @@
 def sum_blocks(id_ref, got_ref, outs, hot):
     tile = lax.broadcasted_iota(jnp.int32, (4 * TILES, PIX), 0)
     for k in range(ALL_BLOCKS // PIX):
-        hot[:, k * PIX : (k + 1) * PIX] = jnp.where(id_ref[k : k + 1, :] == tile, 1.0, 0.0).astype(jnp.bfloat16)
+        hot[:, k * PIX : (k + 1) * PIX] = (id_ref[k : k + 1, :] == tile).astype(jnp.bfloat16)
     halves = [got_ref[:, half * HELD : (half + 1) * HELD, :].reshape(ALL_BLOCKS, PIX) for half in range(2)]
     total = jnp.dot(hot[...], jnp.concatenate(halves, axis=1), preferred_element_type=jnp.float32).astype(jnp.bfloat16)
     for m, out in enumerate(outs):

time: 109 us -> 109 us (level)
  no operation moved by 1% of the time
where the time goes in v6:
time: 109 us
  starting transfers between devices  35.8 us (33%)
  waiting for transfers between devices  27.5 us (25%)
  Pallas kernels  26.8 us (25%)
  blocking collectives  17.1 us (16%)
    ppermute x6, starting transfers between devices, over_z(): return lax.ppermute(part, 'zh', [(i, (i + by) % 4) for i in range(4)])  19.5 us
    pallas_call x1, Pallas kernels, local(): pl.pallas_call(match_blocks, out_shape=jax.ShapeDtypeStruct((GROUP, ROWS,...  18 us
    all_to_all x1, blocking collectives, local(): lax.all_to_all(summed, group, split_axis=0, concat_axis=0, tiled=True)  17.1 us
    all_to_all x1, waiting for transfers between devices, local(): lax.all_to_all(matched_buf, group, split_axis=0, concat_axis=0, tiled=True)  12 us
    all_to_all x1, starting transfers between devices, local(): lax.all_to_all(weight_buf, group, split_axis=0, concat_axis=0, tiled=True)  10.4 us
    ppermute x6, waiting for transfers between devices, over_z(): return lax.ppermute(part, 'zh', [(i, (i + by) % 4) for i in range(4)])  9.78 us
    all_to_all x1, starting transfers between devices, local(): lax.all_to_all(matched_buf, group, split_axis=0, concat_axis=0, tiled=True)  5.9 us
    all_to_all x1, waiting for transfers between devices, local(): lax.all_to_all(weight_buf, group, split_axis=0, concat_axis=0, tiled=True)  5.72 us
  transfers between devices with their start and end apart: 8, of which 4 were waited for; matrix products, arithmetic and copies ran while one was open for 1% of the time, Pallas kernels for 21%

profile of v6, /device:TPU:1, one launch (start us, length us, event | category | flops | bytes accessed | tf_op | source)
XLA Modules:
  0.0 108.9 jit_solution(3764187109330763488)
XLA Ops:
  0.6 2.9 %shard_map.86 = bf16[64,112,128]{2,1,0:T(8,128)(2,1)} custom-call(s32[1]{0:T(128)} %bitcast.zh_ref, s32[1,48]{1,0:T(1,128)} %bitcast.3, s32[1,48]{1,0:T(1,128)} %bitcast.4, bf16[48,128,128]{2,1,0:T(8,128)(2,1)} %var_ref.1), custom_call_target="tpu_custom_call" | custom-call | tf_op jit(solution)/shard_map/pallas_call | solution.py:248
  3.5 0.0 copy-start
  3.5 10.4 %all-to-all-start = ((bf16[64,112,128]{2,1,0:T(8,128)(2,1)}), bf16[64,112,128]{2,1,0:T(8,128)(2,1)S(1)}, u32[]{:S(2)}, u32[]{:S(2)}) async-start(bf16[64,112,128]{2,1,0:T(8,128)(2,1)} %shard_map.86), calls=%async_computation | async-start | bytes 3670016 | tf_op jit(solution)/shard_map/all_to_all | solution.py:266
  13.9 0.0 copy-done
  13.9 0.1 copy.9
  14.0 0.8 reshape.19.coef_ref
  14.8 18.0 %shard_map.89 = bf16[64,96,128]{2,1,0:T(8,128)(2,1)} custom-call(f32[2160]{0:T(1024)} %reshape.19.coef_ref, bf16[48,128,128]{2,1,0:T(8,128)(2,1)} %img_ref.1, bf16[48,128,128]{2,1,0:T(8,128)(2,1)} %var_ref.1, bf16[128,1152]{1,0:T(8,128)(2,1)} %constant.10.clone.xt_ref, bf16[128,1152]{1,0:T(8,128)(2,1)} %constant.11.clone.yt_ref), custom_call_target="tpu_custom_call" | custom-call | flops 6000000000 | bytes 6291456 | tf_op jit(solution)/shard_map/pallas_call | solution.py:267
  32.8 5.7 %all-to-all-done.got_ref = bf16[64,112,128]{2,1,0:T(8,128)(2,1)S(1)} async-done(((bf16[64,112,128]{2,1,0:T(8,128)(2,1)}), bf16[64,112,128]{2,1,0:T(8,128)(2,1)S(1)}, u32[]{:S(2)}, u32[]{:S(2)}) %all-to-all-start) | async-done | bytes 1835040 | tf_op jit(solution)/shard_map/all_to_all | solution.py:266
  38.5 5.9 %all-to-all-start.1 = ((bf16[64,96,128]{2,1,0:T(8,128)(2,1)}), bf16[64,96,128]{2,1,0:T(8,128)(2,1)S(1)}, u32[]{:S(2)}, u32[]{:S(2)}) async-start(bf16[64,96,128]{2,1,0:T(8,128)(2,1)} %shard_map.89), calls=%async_computation.1 | async-start | bytes 3145728 | tf_op jit(solution)/shard_map/all_to_all | solution.py:287
  44.4 2.9 %shard_map.87 = (s32[24,128]{1,0:T(8,128)S(1)}, bf16[256,256]{1,0:T(8,128)(2,1)S(1)}, bf16[256,256]{1,0:T(8,128)(2,1)}, bf16[256,256]{1,0:T(8,128)(2,1)}, bf16[256,256]{1,0:T(8,128)(2,1)}) custom-call(bf16[64,112,128]{2,1,0:T(8,128)(2,1)S(1)} %all-to-all-done.got_ref), custom_call_target="tpu_custom_call" | custom-call | tf_op jit(solution)/shard_map/pallas_call | solution.py:204
  47.3 6.0 %collective-permute-start = (bf16[256,256]{1,0:T(8,128)(2,1)}, bf16[256,256]{1,0:T(8,128)(2,1)S(1)}, u32[]{:S(2)}, u32[]{:S(2)}) collective-permute-start(bf16[256,256]{1,0:T(8,128)(2,1)} %get-tuple-element.12), channel_id=1, source_target_pairs={{0,32},{16,48},{32,0},{48,16},{1,33},{17,49},{33,1},{49,17},{2,34}... | collective-permute-start | bytes 393224 | tf_op jit(solution)/shard_map/ppermute | solution.py:215
  53.3 1.2 %collective-permute-start.1 = (bf16[256,256]{1,0:T(8,128)(2,1)}, bf16[256,256]{1,0:T(8,128)(2,1)S(1)}, u32[]{:S(2)}, u32[]{:S(2)}) collective-permute-start(bf16[256,256]{1,0:T(8,128)(2,1)} %get-tuple-element.13), channel_id=1, source_target_pairs={{0,16},{16,32},{32,48},{48,0},{1,17},{17,33},{33,49},{49,1},{2,18}... | collective-permute-start | bytes 393224 | tf_op jit(solution)/shard_map/ppermute | solution.py:215
  54.5 2.4 %collective-permute-start.2 = (bf16[256,256]{1,0:T(8,128)(2,1)}, bf16[256,256]{1,0:T(8,128)(2,1)S(1)}, u32[]{:S(2)}, u32[]{:S(2)}) collective-permute-start(bf16[256,256]{1,0:T(8,128)(2,1)} %get-tuple-element.14), channel_id=1, source_target_pairs={{0,48},{16,0},{32,16},{48,32},{1,49},{17,1},{33,17},{49,33},{2,50}... | collective-permute-start | bytes 393224 | tf_op jit(solution)/shard_map/ppermute | solution.py:215
  56.9 12.0 %all-to-all-done.1.got_ref = bf16[64,96,128]{2,1,0:T(8,128)(2,1)S(1)} async-done(((bf16[64,96,128]{2,1,0:T(8,128)(2,1)}), bf16[64,96,128]{2,1,0:T(8,128)(2,1)S(1)}, u32[]{:S(2)}, u32[]{:S(2)}) %all-to-all-start.1) | async-done | bytes 1572896 | tf_op jit(solution)/shard_map/all_to_all | solution.py:287
  68.9 2.0 %shard_map.90 = (bf16[256,256]{1,0:T(8,128)(2,1)S(1)}, bf16[256,256]{1,0:T(8,128)(2,1)S(1)}, bf16[256,256]{1,0:T(8,128)(2,1)S(1)}, bf16[256,256]{1,0:T(8,128)(2,1)S(1)}) custom-call(s32[24,128]{1,0:T(8,128)S(1)} %get-tuple-element.15.id_ref, bf16[64,96,128]{2,1,0:T(8,128)(2,1)S(1)} %all-to-all-done.1.got_ref), custom_call_target="tpu_custom_call" | custom-call | tf_op jit(solution)/shard_map/pallas_call | solution.py:196
  70.9 6.1 %collective-permute-start.3 = (bf16[256,256]{1,0:T(8,128)(2,1)S(1)}, bf16[256,256]{1,0:T(8,128)(2,1)S(1)}, u32[]{:S(2)}, u32[]{:S(2)}) collective-permute-start(bf16[256,256]{1,0:T(8,128)(2,1)S(1)} %get-tuple-element.17), channel_id=1, source_target_pairs={{0,32},{16,48},{32,0},{48,16},{1,33},{17,49},{33,1},{49,17},{2,34}... | collective-permute-start | bytes 393224 | tf_op jit(solution)/shard_map/ppermute | solution.py:215
  77.0 3.8 %collective-permute-start.4 = (bf16[256,256]{1,0:T(8,128)(2,1)S(1)}, bf16[256,256]{1,0:T(8,128)(2,1)S(1)}, u32[]{:S(2)}, u32[]{:S(2)}) collective-permute-start(bf16[256,256]{1,0:T(8,128)(2,1)S(1)} %get-tuple-element.18), channel_id=1, source_target_pairs={{0,16},{16,32},{32,48},{48,0},{1,17},{17,33},{33,49},{49,1},{2,18}... | collective-permute-start | bytes 393224 | tf_op jit(solution)/shard_map/ppermute | solution.py:215
  80.8 0.0 collective-permute-done.b_ref
  80.8 0.0 collective-permute-start.5
  80.8 0.0 collective-permute-done.1.c_ref
  80.8 0.0 collective-permute-done.2.d_ref
  80.9 0.1 shard_map.88.depth_ref
  80.9 2.4 %collective-permute-done.3.b_ref = bf16[256,256]{1,0:T(8,128)(2,1)S(1)} collective-permute-done((bf16[256,256]{1,0:T(8,128)(2,1)S(1)}, bf16[256,256]{1,0:T(8,128)(2,1)S(1)}, u32[]{:S(2)}, u32[]{:S(2)}) %collective-permute-start.3) | collective-permute-done | bytes 131104 | tf_op jit(solution)/shard_map/ppermute | solution.py:215
  83.3 7.4 %collective-permute-done.4.c_ref = bf16[256,256]{1,0:T(8,128)(2,1)S(1)} collective-permute-done((bf16[256,256]{1,0:T(8,128)(2,1)S(1)}, bf16[256,256]{1,0:T(8,128)(2,1)S(1)}, u32[]{:S(2)}, u32[]{:S(2)}) %collective-permute-start.4) | collective-permute-done | bytes 131104 | tf_op jit(solution)/shard_map/ppermute | solution.py:215
  90.7 0.0 collective-permute-done.5.d_ref
  90.7 0.2 shard_map.91
  90.9 17.1 %all_to_all.15.got_ref = bf16[64,16,128]{2,1,0:T(8,128)(2,1)S(1)} all-to-all(bf16[64,16,128]{2,1,0:T(8,128)(2,1)S(1)} %shard_map.91), channel_id=1, replica_groups=mesh['x'=4,'zh'=4,'zl'=2,'c'=2,'y'=4] {'zl','c','x','y'}, dimensions={0} | all-to-all | bytes 524288 | tf_op jit(solution)/shard_map/all_to_all | solution.py:305
  108.0 0.9 shard_map.92
Async XLA Ops:
  3.5 10.4 %copy-start = (f32[48,3,15]{0,2,1:T(8,128)S(1)}, f32[48,3,15]{0,2,1:T(8,128)}, u32[]{:S(2)}) copy-start(f32[48,3,15]{0,2,1:T(8,128)} %param.9) | copy-start | bytes 25924
  3.5 35.0 %all-to-all-start = ((bf16[64,112,128]{2,1,0:T(8,128)(2,1)}), bf16[64,112,128]{2,1,0:T(8,128)(2,1)S(1)}, u32[]{:S(2)}, u32[]{:S(2)}) async-start(bf16[64,112,128]{2,1,0:T(8,128)(2,1)} %shard_map.86), calls=%async_computation | async-start | bytes 3670016 | tf_op jit(solution)/shard_map/all_to_all | solution.py:266
  38.5 30.4 %all-to-all-start.1 = ((bf16[64,96,128]{2,1,0:T(8,128)(2,1)}), bf16[64,96,128]{2,1,0:T(8,128)(2,1)S(1)}, u32[]{:S(2)}, u32[]{:S(2)}) async-start(bf16[64,96,128]{2,1,0:T(8,128)(2,1)} %shard_map.89), calls=%async_computation.1 | async-start | bytes 3145728 | tf_op jit(solution)/shard_map/all_to_all | solution.py:287
  47.3 33.5 %collective-permute-start = (bf16[256,256]{1,0:T(8,128)(2,1)}, bf16[256,256]{1,0:T(8,128)(2,1)S(1)}, u32[]{:S(2)}, u32[]{:S(2)}) collective-permute-start(bf16[256,256]{1,0:T(8,128)(2,1)} %get-tuple-element.12), channel_id=1, source_target_pairs={{0,32},{16,48},{32,0},{48,16},{1,33},{17,49},{33,1},{49,17},{2,34}... | collective-permute-start | bytes 393224 | tf_op jit(solution)/shard_map/ppermute | solution.py:215
  53.3 27.5 %collective-permute-start.1 = (bf16[256,256]{1,0:T(8,128)(2,1)}, bf16[256,256]{1,0:T(8,128)(2,1)S(1)}, u32[]{:S(2)}, u32[]{:S(2)}) collective-permute-start(bf16[256,256]{1,0:T(8,128)(2,1)} %get-tuple-element.13), channel_id=1, source_target_pairs={{0,16},{16,32},{32,48},{48,0},{1,17},{17,33},{33,49},{49,1},{2,18}... | collective-permute-start | bytes 393224 | tf_op jit(solution)/shard_map/ppermute | solution.py:215
  54.5 26.3 %collective-permute-start.2 = (bf16[256,256]{1,0:T(8,128)(2,1)}, bf16[256,256]{1,0:T(8,128)(2,1)S(1)}, u32[]{:S(2)}, u32[]{:S(2)}) collective-permute-start(bf16[256,256]{1,0:T(8,128)(2,1)} %get-tuple-element.14), channel_id=1, source_target_pairs={{0,48},{16,0},{32,16},{48,32},{1,49},{17,1},{33,17},{49,33},{2,50}... | collective-permute-start | bytes 393224 | tf_op jit(solution)/shard_map/ppermute | solution.py:215
  70.9 12.4 %collective-permute-start.3 = (bf16[256,256]{1,0:T(8,128)(2,1)S(1)}, bf16[256,256]{1,0:T(8,128)(2,1)S(1)}, u32[]{:S(2)}, u32[]{:S(2)}) collective-permute-start(bf16[256,256]{1,0:T(8,128)(2,1)S(1)} %get-tuple-element.17), channel_id=1, source_target_pairs={{0,32},{16,48},{32,0},{48,16},{1,33},{17,49},{33,1},{49,17},{2,34}... | collective-permute-start | bytes 393224 | tf_op jit(solution)/shard_map/ppermute | solution.py:215
  77.0 13.7 %collective-permute-start.4 = (bf16[256,256]{1,0:T(8,128)(2,1)S(1)}, bf16[256,256]{1,0:T(8,128)(2,1)S(1)}, u32[]{:S(2)}, u32[]{:S(2)}) collective-permute-start(bf16[256,256]{1,0:T(8,128)(2,1)S(1)} %get-tuple-element.18), channel_id=1, source_target_pairs={{0,16},{16,32},{32,48},{48,0},{1,17},{17,33},{33,49},{49,1},{2,18}... | collective-permute-start | bytes 393224 | tf_op jit(solution)/shard_map/ppermute | solution.py:215
  80.8 9.9 %collective-permute-start.5 = (bf16[256,256]{1,0:T(8,128)(2,1)S(1)}, bf16[256,256]{1,0:T(8,128)(2,1)S(1)}, u32[]{:S(2)}, u32[]{:S(2)}) collective-permute-start(bf16[256,256]{1,0:T(8,128)(2,1)S(1)} %get-tuple-element.19), channel_id=1, source_target_pairs={{0,48},{16,0},{32,16},{48,32},{1,49},{17,1},{33,17},{49,33},{2,50}... | collective-permute-start | bytes 393224 | tf_op jit(solution)/shard_map/ppermute | solution.py:215
